TPU v7x, 128 devices: a whole 4x4x4 slice. The times are simulated.
128 devices in a mesh: dp: 32 (over y, x, core), rep: 4 (over z).
Axes of the slice: x: 4, y: 4, z: 4, core: 2. Of those that a mesh axis runs over, the one named last changes fastest.
Arguments:
- tokens: bfloat16 [512, 512, 1024], P(('dp', 'rep')), may hold values from -6 to 6
- token_counts: int32 [512], P(('dp', 'rep')), may hold values from 1 to 512
- segment_ids: int32 [512, 512], P(('dp', 'rep')), may hold values from 0 to 7, never falling along the last dimension, each value on 1 to 128 neighbouring positions
- dest_device: int32 [2048], P(('dp', 'rep')), may hold values from 0 to 31, as said below
- dest_slot: int32 [2048], P(('dp', 'rep')), may hold values from 0 to 15, as said below
- cotangent: bfloat16 [262144, 2048], P(('dp', 'rep')), may hold values from -384 to 384
- master_weight: float32 [1024, 2048], P('dp'), as said below
- momentum: float32 [1024, 2048], replicated, may hold values from -6 to 6
- variance: float32 [1024, 2048], P('dp'), may hold values from 0.25 to 4
Outputs:
- new_weights: bfloat16 [1024, 2048], replicated
- new_momentum: float32 [1024, 2048], P('dp')
- lamb_step: float32 [1024, 2048], P('dp')
Inputs may be any that keep to these rules, and one draw needn't show every extreme that they name: `dest_device`: for each replica group, every block goes to a dp index; one device sends at most 1 block to any one device of its replica group, so its 16 blocks go to 16 different dp indices; every device receives exactly 16 blocks. `dest_slot`: the blocks received by one device have distinct slots, so all 16 slots are filled. `master_weight`: master weights, fan-in scaled, finite.
All inputs are finite; a program needn't handle non-finite values. Where the computation divides by a largest or mean magnitude, that divisor is 1e-20 or more.
Results may differ from a plain program's by a relative error of at most 0.0075.
Values may be sent and summed in bfloat16 or wider, within the bound.
A program may use at most 128 MiB of HBM per device.

v0:
```python
import jax
import jax.numpy as jnp
from jax import lax
from jax.sharding import PartitionSpec as P

root_half = 0.7071067811865476
normal_peak = 0.3989422804014327
momentum_decay = 0.9
learn_rate = 0.05
epsilon = 1e-06


def segment_lengths(segment_ids, token_counts):
    position = lax.broadcasted_iota(jnp.int32, segment_ids.shape, 1)
    living = position < token_counts[:, None]
    matched = (segment_ids[:, :, None] == segment_ids[:, None, :]) & living[:, None, :]
    return jnp.where(living, jnp.sum(matched, axis=2, dtype=jnp.int32), 0)


def gelu_slope(preact):
    return (
        0.5 * (1.0 + lax.erf(preact * root_half))
        + preact * jnp.exp(-0.5 * preact * preact) * normal_peak
    )


def server_step(average, owned_variance):
    row_scale = jnp.mean(jnp.abs(average), axis=1)
    moment = row_scale[:, None] * jnp.tanh(average / (row_scale + epsilon)[:, None])
    return (moment, moment / (jnp.sqrt(owned_variance) + epsilon))


def per_device(
    tokens,
    token_counts,
    segment_ids,
    dest_device,
    dest_slot,
    cotangent,
    master_weight,
    momentum,
    variance,
):
    row_count, seq_length, model_width = tokens.shape
    block_count = dest_device.shape[0]
    block_tokens = row_count * seq_length // block_count
    hidden_width = master_weight.shape[1]
    data_peers = lax.axis_size("dp")
    replicas = lax.axis_size("rep")
    peer_room = max(1, block_count // data_peers)
    lengths = segment_lengths(segment_ids, token_counts).reshape(block_count, block_tokens)
    ordinal = jnp.arange(block_count, dtype=jnp.int32)
    earlier = (dest_device[:, None] == dest_device[None, :]) & (ordinal[None, :] < ordinal[:, None])
    within = jnp.sum(earlier, axis=1, dtype=jnp.int32)
    position = dest_device * peer_room + within
    outgoing = jnp.arange(data_peers * peer_room, dtype=jnp.int32)
    chooser = outgoing[:, None] == position[None, :]
    flat_tokens = tokens.reshape(block_count, block_tokens * model_width)
    send_blocks = jnp.dot(
        chooser.astype(jnp.bfloat16), flat_tokens, preferred_element_type=jnp.float32
    ).astype(jnp.bfloat16)
    chooser_int = chooser.astype(jnp.int32)
    send_slots = jnp.dot(chooser_int, dest_slot + 1) - 1
    send_lengths = jnp.dot(chooser_int, lengths)
    arrived = lax.all_to_all(
        send_blocks.reshape(data_peers, peer_room, block_tokens * model_width),
        "dp",
        split_axis=0,
        concat_axis=0,
        tiled=True,
    )
    arrived_slots, arrived_lengths = (
        lax.all_to_all(
            send_slots.reshape(data_peers, peer_room), "dp", split_axis=0, concat_axis=0, tiled=True
        ),
        lax.all_to_all(
            send_lengths.reshape(data_peers, peer_room, block_tokens),
            "dp",
            split_axis=0,
            concat_axis=0,
            tiled=True,
        ),
    )
    placer = arrived_slots.reshape(-1)[None, :] == ordinal[:, None]
    local_tokens = (
        jnp.dot(
            placer.astype(jnp.bfloat16),
            arrived.reshape(data_peers * peer_room, block_tokens * model_width),
            preferred_element_type=jnp.float32,
        )
        .astype(jnp.bfloat16)
        .reshape(block_count * block_tokens, model_width)
    )
    local_lengths = jnp.dot(
        placer.astype(jnp.int32), arrived_lengths.reshape(data_peers * peer_room, block_tokens)
    ).reshape(-1)
    token_weight = jnp.where(
        local_lengths > 0, 1.0 / jnp.maximum(local_lengths, 1).astype(jnp.float32), 0.0
    )
    preact = jnp.dot(
        local_tokens,
        lax.all_gather(master_weight.astype(jnp.bfloat16), "dp", axis=0, tiled=True),
        preferred_element_type=jnp.float32,
    )
    delta = (cotangent.astype(jnp.float32) * gelu_slope(preact) * token_weight[:, None]).astype(
        jnp.bfloat16
    )
    grad = lax.dot_general(
        local_tokens, delta, (((0,), (0,)), ((), ())), preferred_element_type=jnp.float32
    )
    moment = momentum_decay * momentum + (1.0 - momentum_decay) * grad
    row_scale = jnp.mean(jnp.abs(moment), axis=1)
    unit = jnp.tanh(moment / (row_scale + epsilon)[:, None]).astype(jnp.bfloat16)
    sent_scale = row_scale.astype(jnp.bfloat16)
    owned_units, owned_scales = (
        lax.all_to_all(
            unit.reshape(data_peers, -1, hidden_width),
            "dp",
            split_axis=0,
            concat_axis=0,
            tiled=True,
        ),
        lax.all_to_all(
            sent_scale.reshape(data_peers, -1), "dp", split_axis=0, concat_axis=0, tiled=True
        ),
    )
    partial_sum = jnp.sum(
        owned_units.astype(jnp.float32) * owned_scales.astype(jnp.float32)[:, :, None], axis=0
    )
    average = lax.psum(partial_sum.astype(jnp.bfloat16), "rep").astype(jnp.float32) / (
        data_peers * replicas
    )
    new_momentum, direction = server_step(average, variance)
    weight_square, direction_square = lax.psum(
        (jnp.sum(master_weight * master_weight), jnp.sum(direction * direction)), "dp"
    )
    ratio = jnp.sqrt(weight_square) / (jnp.sqrt(direction_square) + epsilon)
    lamb_step = ratio * direction
    fresh = (master_weight - learn_rate * lamb_step).astype(jnp.bfloat16)
    new_weights = lax.all_gather(fresh, "dp", axis=0, tiled=True)
    return (new_weights, new_momentum, lamb_step)


def solution(mesh):
    return jax.shard_map(
        per_device,
        mesh=mesh,
        in_specs=(
            P(("dp", "rep"), None, None),
            P(("dp", "rep")),
            P(("dp", "rep"), None),
            P(("dp", "rep")),
            P(("dp", "rep")),
            P(("dp", "rep"), None),
            P("dp", None),
            P(),
            P("dp", None),
        ),
        out_specs=(P(), P("dp", None), P("dp", None)),
        check_vma=False,
    )
```

profile of v0, /device:TPU:1, one launch (start us, length us, event | category | flops | bytes accessed | tf_op | source)
XLA Modules:
  0.0 503.5 jit_solution(13465399309310281165)
XLA Ops:
  10.2 8.6 %all-to-all-start = ((s32[32,1,1]{2,1,0:T(1,128)}), s32[32,1,1]{2,1,0:T(1,128)S(1)}, u32[]{:S(2)}, u32[]{:S(2)}) async-start(s32[32,1,1]{2,1,0:T(1,128)} %copy.19), calls=%async_computation | async-start | bytes 32768 | tf_op jit(solution)/shard_map/all_to_all | solution.py:73
  19.6 1.7 convert_reduce_fusion
  22.9 4.8 reshape.116
  27.7 7.4 %all-to-all-start.2 = ((s32[32,1,128]{2,1,0:T(1,128)}), s32[32,1,128]{2,1,0:T(1,128)S(1)}, u32[]{:S(2)}, u32[]{:S(2)}) async-start(s32[32,1,128]{2,1,0:T(1,128)} %bitcast.6), calls=%async_computation.2 | async-start | bytes 32768 | tf_op jit(solution)/shard_map/all_to_all | solution.py:76
  35.1 7.7 %fusion = bf16[32,1,131072]{2,0,1:T(8,128)(2,1)} fusion(bf16[16,131072]{1,0:T(8,128)(2,1)} %reshape.116, s32[16]{0:T(128)S(1)} %add.55), kind=kOutput, calls=%fused_computation.1 | convolution fusion | flops 138412544 | bytes 12582976 | tf_op jit(solution)/shard_map/dot_general | solution.py:59
  43.4 11.5 %reduce.1 = bf16[32,131072]{1,0:T(8,128)(2,1)} reduce(bf16[32,1,131072]{2,0,1:T(8,128)(2,1)} %fusion, bf16[]{:T(256)} %broadcast.89), dimensions={1}, to_apply=%copy.20.reduce_sub_computation | reduce | bytes 16777218 | tf_op jit(solution)/shard_map/reshape | solution.py:66
  54.8 11.0 %reshape.127 = bf16[32,2,65536]{2,1,0:T(2,128)(2,1)} reshape(bf16[32,131072]{1,0:T(8,128)(2,1)} %reduce.1) | data formatting | bytes 16777216
  65.8 7.6 %all-to-all-start.1 = ((bf16[32,2,65536]{2,1,0:T(2,128)(2,1)}), bf16[32,2,65536]{2,1,0:T(2,128)(2,1)}, u32[]{:S(2)}, u32[]{:S(2)}) async-start(bf16[32,2,65536]{2,1,0:T(2,128)(2,1)} %reshape.127), calls=%async_computation.1 | async-start | bytes 16777216 | tf_op jit(solution)/shard_map/all_to_all | solution.py:65
  75.7 102.0 %all-to-all-done.1 = bf16[32,2,65536]{2,1,0:T(2,128)(2,1)} async-done(((bf16[32,2,65536]{2,1,0:T(2,128)(2,1)}), bf16[32,2,65536]{2,1,0:T(2,128)(2,1)}, u32[]{:S(2)}, u32[]{:S(2)}) %all-to-all-start.1) | async-done | bytes 8388640 | tf_op jit(solution)/shard_map/all_to_all | solution.py:65
  177.7 23.4 %reshape.128 = bf16[32,1,131072]{2,1,0:T(2,128)(2,1)} reshape(bf16[32,2,65536]{2,1,0:T(2,128)(2,1)} %all-to-all-done.1) | data formatting | bytes 16777216
  201.1 16.9 %convolution_convert_fusion.1 = bf16[16,131072]{1,0:T(8,128)(2,1)} fusion(bf16[32,1,131072]{2,1,0:T(2,128)(2,1)} %reshape.128, s32[32]{0:T(128)S(1)} %reduce), kind=kOutput, calls=%fused_computation.2 | convolution fusion | flops 136315392 | bytes 12583040 | tf_op jit(solution)/shard_map/dot_general | solution.py:86
  218.0 4.8 reshape.119
  222.8 18.7 %fusion.15.clone.4 = bf16[2048,2048]{1,0:T(8,128)(2,1)S(1)} fusion(bf16[2048,2048]{1,0:T(8,128)(2,1)} %param.14, f32[2048]{0:T(1024)S(1)} %select_bitcast_fusion, bf16[2048,1024]{1,0:T(8,128)(2,1)} %reshape.119, bf16[1024,2048]{1,0:T(8,128)(2,1)} %all-gather.3.cloned.1.call-done), kind=kOutput, calls=%fused_computation.10.clone.clone.clone.clone.clone.clone.1 | convolution fusion | flops 8640266240 | bytes 25174016 | tf_op jit(solution)/shard_map/dot_general | solution.py:100
  241.6 13.5 %abs_reduce_fusion = (f32[1024]{0:T(1024)S(1)}, f32[1024,2048]{1,0:T(8,128)}) fusion(bf16[2048,1024]{1,0:T(8,128)(2,1)S(1)} %copy-done, f32[1024,2048]{1,0:T(8,128)} %param.16, bf16[2048,2048]{1,0:T(8,128)(2,1)S(1)} %fusion.15.clone.4), kind=kOutput, calls=%fused_computation.15 | convolution fusion | flops 8600419328 | bytes 29364224 | tf_op jit(solution)/shard_map/dot_general | solution.py:108
  255.7 14.2 %all-to-all-start.4 = ((bf16[32,1,32]{2,1,0:T(2,128)(2,1)}), bf16[32,1,32]{2,1,0:T(2,128)(2,1)S(1)}, u32[]{:S(2)}, u32[]{:S(2)}) async-start(bf16[32,1,32]{2,1,0:T(2,128)(2,1)} %convert_element_type.90), calls=%async_computation.4 | async-start | bytes 32768 | tf_op jit(solution)/shard_map/all_to_all | solution.py:123
  269.9 5.7 %tanh_convert_fusion = bf16[1024,2048]{1,0:T(8,128)(2,1)} fusion(f32[1024,2048]{1,0:T(8,128)} %get-tuple-element.16, f32[1024]{0:T(1024)S(1)} %get-tuple-element.12), kind=kLoop, calls=%fused_computation.14 | loop fusion | flops 4194304 | bytes 12587008 | tf_op jit(solution)/shard_map/convert_element_type | solution.py:113
  276.9 6.4 %all-to-all-start.3 = ((bf16[32,32,2048]{2,1,0:T(8,128)(2,1)}), bf16[32,32,2048]{2,1,0:T(8,128)(2,1)}, u32[]{:S(2)}, u32[]{:S(2)}) async-start(bf16[32,32,2048]{2,1,0:T(8,128)(2,1)} %bitcast.38), calls=%async_computation.3 | async-start | bytes 8388608 | tf_op jit(solution)/shard_map/all_to_all | solution.py:116
  283.3 50.2 %all-to-all-done.3 = bf16[32,32,2048]{2,1,0:T(8,128)(2,1)} async-done(((bf16[32,32,2048]{2,1,0:T(8,128)(2,1)}), bf16[32,32,2048]{2,1,0:T(8,128)(2,1)}, u32[]{:S(2)}, u32[]{:S(2)}) %all-to-all-start.3) | async-done | bytes 4194336 | tf_op jit(solution)/shard_map/all_to_all | solution.py:116
  333.5 3.7 multiply_reduce_fusion
  337.3 40.0 %all-reduce.3.cloned.1.call-done = bf16[32,2048]{1,0:T(8,128)(2,1)} async-done(((bf16[32,2048]{1,0:T(8,128)(2,1)}), bf16[32,2048]{1,0:T(8,128)(2,1)}) %all-reduce.3.cloned.1.call-update) | async-done | bytes 131088 | tf_op jit(solution)/shard_map/psum | solution.py:130
  378.4 1.7 multiply_reduce_fusion.1
  380.1 65.4 %all-reduce = (f32[]{:T(128)}, f32[]{:T(128)}) all-reduce(f32[]{:T(128)} %get-tuple-element.9, f32[]{:T(128)} %get-tuple-element.7), channel_id=1, replica_groups=mesh['dp'=32,'rep'=4] {'dp'}, use_global_device_ids=true, to_apply=%region_1.2 | all-reduce | flops 2 | bytes 16 | tf_op jit(solution)/shard_map/psum | solution.py:134
  447.8 44.4 %all-gather.5.cloned.1.call-done = bf16[1024,2048]{1,0:T(8,128)(2,1)} async-done(((bf16[32,2048]{1,0:T(8,128)(2,1)}), bf16[1024,2048]{1,0:T(8,128)(2,1)}) %all-gather.5.cloned.1.call-update) | async-done | bytes 4194320 | tf_op jit(solution)/shard_map/all_gather | solution.py:140
  492.1 4.8 copy.31
  (39 shorter events, 12.3 us)
Async XLA Ops:
  10.2 17.5 %all-to-all-start = ((s32[32,1,1]{2,1,0:T(1,128)}), s32[32,1,1]{2,1,0:T(1,128)S(1)}, u32[]{:S(2)}, u32[]{:S(2)}) async-start(s32[32,1,1]{2,1,0:T(1,128)} %copy.19), calls=%async_computation | async-start | bytes 32768 | tf_op jit(solution)/shard_map/all_to_all | solution.py:73
  27.7 38.1 %all-to-all-start.2 = ((s32[32,1,128]{2,1,0:T(1,128)}), s32[32,1,128]{2,1,0:T(1,128)S(1)}, u32[]{:S(2)}, u32[]{:S(2)}) async-start(s32[32,1,128]{2,1,0:T(1,128)} %bitcast.6), calls=%async_computation.2 | async-start | bytes 32768 | tf_op jit(solution)/shard_map/all_to_all | solution.py:76
  65.8 7.8 %copy-start.1 = (f32[32,2048]{1,0:T(8,128)S(1)}, f32[32,2048]{1,0:T(8,128)}, u32[]{:S(2)}) copy-start(f32[32,2048]{1,0:T(8,128)} %param.15) | copy-start | bytes 786436
  65.8 111.9 %all-to-all-start.1 = ((bf16[32,2,65536]{2,1,0:T(2,128)(2,1)}), bf16[32,2,65536]{2,1,0:T(2,128)(2,1)}, u32[]{:S(2)}, u32[]{:S(2)}) async-start(bf16[32,2,65536]{2,1,0:T(2,128)(2,1)} %reshape.127), calls=%async_computation.1 | async-start | bytes 16777216 | tf_op jit(solution)/shard_map/all_to_all | solution.py:65
  73.4 149.4 %all-gather.3.cloned.1.call-start = ((), (), s32[]{:S(2)}) async-start(), calls=%async_computation.5 | async-start | bytes 4325376 | tf_op jit(solution)/shard_map/all_gather | solution.py:102
  222.8 18.7 %copy-start = (bf16[2048,1024]{1,0:T(8,128)(2,1)S(1)}, bf16[2048,1024]{1,0:T(8,128)(2,1)}, u32[]{:S(2)}) copy-start(bf16[2048,1024]{1,0:T(8,128)(2,1)} %reshape.119) | copy-start | bytes 12582916
  255.7 21.1 %all-to-all-start.4 = ((bf16[32,1,32]{2,1,0:T(2,128)(2,1)}), bf16[32,1,32]{2,1,0:T(2,128)(2,1)S(1)}, u32[]{:S(2)}, u32[]{:S(2)}) async-start(bf16[32,1,32]{2,1,0:T(2,128)(2,1)} %convert_element_type.90), calls=%async_computation.4 | async-start | bytes 32768 | tf_op jit(solution)/shard_map/all_to_all | solution.py:123
  275.5 102.8 %copy-start.2 = (f32[32,2048]{1,0:T(8,128)S(1)}, f32[32,2048]{1,0:T(8,128)}, u32[]{:S(2)}) copy-start(f32[32,2048]{1,0:T(8,128)} %param.17) | copy-start | bytes 786436
  276.9 56.6 %all-to-all-start.3 = ((bf16[32,32,2048]{2,1,0:T(8,128)(2,1)}), bf16[32,32,2048]{2,1,0:T(8,128)(2,1)}, u32[]{:S(2)}, u32[]{:S(2)}) async-start(bf16[32,32,2048]{2,1,0:T(8,128)(2,1)} %bitcast.38), calls=%async_computation.3 | async-start | bytes 8388608 | tf_op jit(solution)/shard_map/all_to_all | solution.py:116
  283.2 94.1 %all-reduce.3.cloned.1.call-start = ((), (), s32[]{:S(2)}) async-start(), calls=%async_computation.6 | async-start | bytes 262144 | tf_op jit(solution)/shard_map/psum | solution.py:130
  337.3 154.9 %all-gather.5.cloned.1.call-start = ((), (), s32[]{:S(2)}) async-start(), calls=%async_computation.7 | async-start | bytes 4325376 | tf_op jit(solution)/shard_map/all_gather | solution.py:140
  380.1 116.9 %copy-start.3 = (f32[32,2048]{1,0:T(8,128)}, f32[32,2048]{1,0:T(8,128)S(1)}, u32[]{:S(2)}) copy-start(f32[32,2048]{1,0:T(8,128)S(1)} %get-tuple-element.21) | copy-start | bytes 786436
Sparse Core Ops, SparseCore 0:
  77.1 107.9 all-gather.2
  337.4 39.8 all-reduce.2
  447.9 44.2 all-gather.4
where the time goes:
time: 505 us; the launch traced here: 503 us
  waiting for transfers between devices  238 us (47%)
  blocking collectives  65.4 us (13%)
  matrix products  58.5 us (12%)
  local copies, waits for them, and re-layouts  51.5 us (10%)
  starting transfers between devices  44.4 us (9%)
  other arithmetic  30.4 us (6%)
  between operations  15.3 us (3%)
    all_to_all x1, waiting for transfers between devices, per_device(): lax.all_to_all(send_blocks.reshape(data_peers, peer_room, block_tokens *...  102 us
    psum x1, blocking collectives, per_device(): lax.psum((jnp.sum(master_weight * master_weight), jnp.sum(direction * dir...  65.4 us
    all_to_all x1, waiting for transfers between devices, per_device(): lax.all_to_all(unit.reshape(data_peers, -1, hidden_width), 'dp', split_ax...  50.2 us
    all_gather x1, waiting for transfers between devices, per_device(): new_weights = lax.all_gather(fresh, 'dp', axis=0, tiled=True)  44.4 us
    psum x1, waiting for transfers between devices, per_device(): lax.psum(partial_sum.astype(jnp.bfloat16), 'rep').astype(jnp.float32)  40 us
    unnamed x11, local copies, waits for them, and re-layouts  39.2 us
    dot_general x1, matrix products, per_device(): jnp.dot(local_tokens, lax.all_gather(master_weight.astype(jnp.bfloat16),...  18.7 us
    dot_general x1, matrix products, per_device(): jnp.dot(placer.astype(jnp.bfloat16), arrived.reshape(data_peers * peer_ro...  16.9 us
  transfers between devices with their start and end apart: 8, of which 5 were waited for; matrix products, arithmetic and copies ran while one was open for 18% of the time, Pallas kernels for 0%

commit v1 on v0

v1 whole, which is shorter than its diff:
```python
import functools

import jax
import jax.numpy as jnp
from jax import lax
from jax.experimental import pallas as pl
from jax.experimental.pallas import tpu as pltpu
from jax.sharding import PartitionSpec as P

MESH = pl.DeviceIdType.MESH
F32 = jnp.float32
BF16 = jnp.bfloat16
momentum_decay = 0.9
learn_rate = 0.05
epsilon = 1e-06
normal_peak = 0.3989422804014327

GROUPS = (
    ((0, 1), (0, 3), (1, 0), (3, 0)),
    ((1, 1), (3, 3)),
    ((1, 3), (3, 1)),
    ((0, 2), (2, 0)),
    ((1, 2), (3, 2), (2, 1), (2, 3)),
    ((2, 2),),
)
MOVES = [(0, 0, 0), (0, 0, 1)]
for group in GROUPS:
    for core in (0, 1):
        for dy, dx in group:
            MOVES.append((dy, dx, core))

PER = 4
TILE = 256


def gelu_slope(a):
    u = jnp.abs(a)
    t = 1.0 / (1.0 + u * (0.3275911 * 0.7071067811865476))
    e = jnp.exp(-0.5 * (a * a))
    poly = t * (
        0.5 * 0.254829592
        + t
        * (
            0.5 * -0.284496736
            + t * (0.5 * 1.421413741 + t * (0.5 * -1.453152027 + t * (0.5 * 1.061405429)))
        )
    )
    h = e * (poly - normal_peak * u)
    return jnp.where(a >= 0.0, 1.0 - h, h)


def kernel(
    inv,
    tok_hbm,
    meta,
    cot_hbm,
    master,
    mom_hbm,
    variance,
    out_w,
    out_m,
    out_l,
    tok,
    stage,
    arr,
    cot,
    w,
    acc,
    xt,
    wt,
    metar,
    metas,
    u,
    r1,
    s1,
    r2,
    s2,
    r3,
    r4,
    dirs,
    q,
    lsem,
    tss,
    tsr,
    mss,
    msr,
    gbs,
    gbr,
    gas,
    gar,
    gcs,
    gcr,
    c1s,
    c1r,
    c2s,
    c2r,
    c3s,
    c3r,
    c4s,
    c4r,
    qs,
    qr,
):
    me = lax.axis_index("dp")
    rep = lax.axis_index("rep")
    y = me // 8
    x = (me // 2) % 4
    c = me % 2
    a = (1 - c) * y + c * x
    b = (1 - c) * x + c * y
    sa = 4 * (1 - c) + c
    sb = 4 * c + (1 - c)

    def place(ai, bi):
        return ai * sa + bi * sb

    def copy(src, dst, ss, rs, dev):
        return pltpu.make_async_remote_copy(
            src_ref=src, dst_ref=dst, send_sem=ss, recv_sem=rs, device_id=dev, device_id_type=MESH
        )

    def peer(move):
        dy, dx, dc = move
        return (((y + dy) % 4) * 4 + (x + dx) % 4) * 2 + (c + dc) % 2

    ctok = pltpu.make_async_copy(tok_hbm, tok, lsem.at[0])
    ccot = pltpu.make_async_copy(cot_hbm, cot, lsem.at[1])
    cmom = pltpu.make_async_copy(mom_hbm, acc, lsem.at[2])
    ctok.start()

    barrier = pltpu.get_barrier_semaphore()

    @pl.loop(1, 32)
    def _(k):
        pl.semaphore_signal(barrier, inc=1, device_id=((me + k) % 32, rep), device_id_type=MESH)

    for k in range(1, 4):
        pl.semaphore_signal(barrier, inc=1, device_id=(me, (rep + k) % 4), device_id_type=MESH)
    w[y * 4 + x, c] = master[...].astype(BF16)
    pl.semaphore_wait(barrier, 34)

    def gather_b(g):
        out = []
        for k in range(1, 4):
            mine = w.at[y * 4 + x, c]
            cp = copy(
                mine, mine, gbs.at[g, k - 1], gbr.at[g, k - 1],
                (place(a, (b + k) % 4) * 2 + c, rep),
            )
            cp.start()
            out.append(cp)
        return out

    def gather_a(g):
        out = []
        for k in range(1, 4):
            for bb in range(4):
                part = w.at[place(a, bb), c]
                cp = copy(
                    part, part, gas.at[g, k - 1, bb], gar.at[g, k - 1, bb],
                    (place((a + k) % 4, b) * 2 + c, rep),
                )
                cp.start()
                out.append(cp)
        return out

    def gather_c(g):
        part = w.at[:, c]
        cp = copy(part, part, gcs.at[g], gcr.at[g], (y * 8 + x * 2 + 1 - c, rep))
        cp.start()
        return [cp]

    first = gather_b(0)

    metacopies = []
    for j in range(1, 32):
        p = peer(MOVES[j])
        cp = copy(meta.at[p], metar.at[j], mss.at[j], msr.at[j], (p, rep))
        cp.start()
        metacopies.append(cp)
    metar[0] = meta[me]

    ctok.wait()
    ccot.start()
    cmom.start()
    sends = []

    def send(j):
        p = peer(MOVES[j])
        stage[j] = tok[inv[p]]
        cp = copy(stage.at[j], arr.at[j], tss.at[j], tsr.at[j], (p, rep))
        cp.start()
        sends.append(cp)

    arr[0] = tok[inv[me]]
    for j in range(1, 4):
        send(j)
    for cp in first:
        cp.wait()
    second = gather_a(0)
    for j in range(4, 32):
        send(j)
    for cp in metacopies:
        cp.wait()
    cmeta = pltpu.make_async_copy(metar, metas, lsem.at[3])
    cmeta.start()
    for cp in second:
        cp.wait()
    third = gather_c(0)
    cmom.wait()

    @pl.loop(0, 32)
    def _(i):
        rows = pl.ds(pl.multiple_of(i * 32, 32), 32)
        acc[rows, :] = acc[rows, :] * (momentum_decay / (1.0 - momentum_decay))

    cmeta.wait()
    ccot.wait()
    for cp in third:
        cp.wait()

    def work(ch):
        for i in range(PER):
            j = ch * PER + i
            lens = metar[j][0:1, :]
            weight = jnp.where(lens > 0, 1.0 / jnp.maximum(lens, 1).astype(F32), 0.0)
            wt[i * 128 : (i + 1) * 128, :] = jnp.transpose(jnp.broadcast_to(weight, (128, 128)))
            xt[:, i * 128 : (i + 1) * 128] = jnp.transpose(arr[j])

        @pl.loop(0, 2048 // TILE)
        def _(n):
            cols = pl.ds(pl.multiple_of(n * TILE, TILE), TILE)
            xin = arr[pl.ds(ch * PER, PER)].reshape(PER * 128, 1024)
            pre = jnp.dot(xin, w[:, :, :, cols].reshape(1024, TILE), preferred_element_type=F32)
            parts = []
            for i in range(PER):
                slot = metas[ch * PER + i, 1, 0]
                ci = cot[slot, :, cols].astype(F32)
                rows = slice(i * 128, (i + 1) * 128)
                wcol = wt[rows, :]
                wide = jnp.concatenate([wcol] * (TILE // 128), axis=1)
                parts.append((ci * gelu_slope(pre[rows]) * wide).astype(BF16))
            delta = jnp.concatenate(parts, axis=0)
            acc[:, cols] += jnp.dot(xt[...], delta, preferred_element_type=F32)

    for i in range(1, PER):
        sends[i - 1].wait_recv()
    work(0)

    @pl.loop(1, 32 // PER)
    def _(ch):
        for i in range(PER):
            j = ch * PER + i
            copy(stage.at[j], arr.at[j], tss.at[j], tsr.at[j], (me, (rep + 1) % 4)).wait_recv()
        work(ch)

    for cp in sends:
        cp.wait_send()

    def squeezed(yx, core):
        rows = pl.ds(pl.multiple_of((yx * 2 + core) * 32, 32), 32)
        moment = acc[rows, :] * (1.0 - momentum_decay)
        scale = jnp.sum(jnp.abs(moment), axis=1, keepdims=True) * (1.0 / 2048)
        unit = jnp.tanh(moment / (scale + epsilon))
        return scale.astype(BF16).astype(F32) * unit.astype(BF16).astype(F32)

    other = (y * 8 + x * 2 + 1 - c, rep)

    @pl.loop(0, 16)
    def _(i):
        yx = place((a + 1 + i // 4) % 4, i % 4)
        u[i] = squeezed(yx, 1 - c).astype(BF16)
        copy(u.at[i], r1.at[yx], c1s.at[i], c1r.at[yx], other).start()

    def add_core(k):
        for bb in range(4):
            yx = place((a + k) % 4, bb)
            copy(u.at[0], r1.at[yx], c1s.at[0], c1r.at[yx], other).wait_recv()
            s1[k, bb] = (squeezed(yx, c) + r1[yx].astype(F32)).astype(BF16)

    stage2 = []
    for k in (2, 1, 3, 0):
        add_core(k)
        if k:
            cp = copy(
                s1.at[k], r2.at[k - 1], c2s.at[k - 1], c2r.at[k - 1],
                (place((a + k) % 4, b) * 2 + c, rep),
            )
            cp.start()
            stage2.append(cp)
    for cp in stage2:
        cp.wait()

    def add_a(bi):
        total = s1[0, bi].astype(F32)
        for k in range(3):
            total = total + r2[k, bi].astype(F32)
        return total

    stage3 = []
    for k in (2, 1, 3):
        bi = (b + k) % 4
        s2[k - 1] = add_a(bi).astype(BF16)
        cp = copy(
            s2.at[k - 1], r3.at[k - 1], c3s.at[k - 1], c3r.at[k - 1],
            (place(a, bi) * 2 + c, rep),
        )
        cp.start()
        stage3.append(cp)
    total = add_a(b)
    for cp in stage3:
        cp.wait()
    for k in range(3):
        total = total + r3[k].astype(F32)
    r4[rep] = total.astype(BF16)
    stage4 = []
    for k in (2, 1, 3):
        cp = copy(
            r4.at[rep], r4.at[rep], c4s.at[k - 1], c4r.at[k - 1], (me, (rep + k) % 4)
        )
        cp.start()
        stage4.append(cp)
    for cp in stage4:
        cp.wait()
    average = (
        r4[0].astype(F32) + r4[1].astype(F32) + r4[2].astype(F32) + r4[3].astype(F32)
    ) * (1.0 / 128)
    scale = jnp.sum(jnp.abs(average), axis=1, keepdims=True) * (1.0 / 2048)
    moment = scale * jnp.tanh(average / (scale + epsilon))
    out_m[...] = moment
    direction = moment / (jnp.sqrt(variance[...]) + epsilon)
    dirs[...] = direction

    def folded(v):
        line = jnp.sum(v, axis=0, keepdims=True)
        out = line[:, 0:128]
        for i in range(1, 16):
            out = out + line[:, i * 128 : (i + 1) * 128]
        return out

    q[me] = jnp.concatenate(
        [
            folded(master[...] * master[...]),
            folded(direction * direction),
            jnp.zeros((6, 128), F32),
        ],
        axis=0,
    )
    scalars = []
    for j in range(1, 32):
        cp = copy(q.at[me], q.at[me], qs.at[j], qr.at[j], (peer(MOVES[j]), rep))
        cp.start()
        scalars.append(cp)
    for cp in scalars:
        cp.wait()
    sums = jnp.sum(jnp.sum(q[...], axis=0), axis=1, keepdims=True)
    roots = jnp.sqrt(sums)
    ratio = roots[0:1, :] / (roots[1:2, :] + epsilon)
    step = ratio * dirs[...]
    out_l[...] = step
    w[y * 4 + x, c] = (master[...] - learn_rate * step).astype(BF16)
    for stagefn in (gather_b, gather_a, gather_c):
        for cp in stagefn(1):
            cp.wait()

    @pl.loop(0, 16)
    def _(i):
        copy(u.at[i], r1.at[i], c1s.at[i], c1r.at[i], other).wait_send()

    cout = pltpu.make_async_copy(w, out_w, lsem.at[4])
    cout.start()
    cout.wait()


def run(inv, tokens, meta, cotangent, master, momentum, variance):
    sem = pltpu.SemaphoreType.DMA
    vmem = pl.BlockSpec(memory_space=pltpu.VMEM)
    hbm = pl.BlockSpec(memory_space=pl.ANY)
    return pl.pallas_call(
        kernel,
        out_shape=(
            jax.ShapeDtypeStruct((16, 2, 32, 2048), BF16),
            jax.ShapeDtypeStruct((32, 2048), F32),
            jax.ShapeDtypeStruct((32, 2048), F32),
        ),
        in_specs=[
            pl.BlockSpec(memory_space=pltpu.SMEM),
            hbm,
            vmem,
            hbm,
            vmem,
            hbm,
            vmem,
        ],
        out_specs=(hbm, vmem, vmem),
        scratch_shapes=[
            pltpu.VMEM((16, 128, 1024), BF16),
            pltpu.VMEM((32, 128, 1024), BF16),
            pltpu.VMEM((32, 128, 1024), BF16),
            pltpu.VMEM((16, 128, 2048), BF16),
            pltpu.VMEM((16, 2, 32, 2048), BF16),
            pltpu.VMEM((1024, 2048), F32),
            pltpu.VMEM((1024, PER * 128), BF16),
            pltpu.VMEM((PER * 128, 128), F32),
            pltpu.VMEM((32, 8, 128), jnp.int32),
            pltpu.SMEM((32, 8, 128), jnp.int32),
            pltpu.VMEM((16, 32, 2048), BF16),
            pltpu.VMEM((16, 32, 2048), BF16),
            pltpu.VMEM((4, 4, 32, 2048), BF16),
            pltpu.VMEM((3, 4, 32, 2048), BF16),
            pltpu.VMEM((3, 32, 2048), BF16),
            pltpu.VMEM((3, 32, 2048), BF16),
            pltpu.VMEM((4, 32, 2048), BF16),
            pltpu.VMEM((32, 2048), F32),
            pltpu.VMEM((32, 8, 128), F32),
            sem((5,)),
            sem((32,)),
            sem((32,)),
            sem((32,)),
            sem((32,)),
            sem((2, 3)),
            sem((2, 3)),
            sem((2, 3, 4)),
            sem((2, 3, 4)),
            sem((2,)),
            sem((2,)),
            sem((16,)),
            sem((16,)),
            sem((3,)),
            sem((3,)),
            sem((3,)),
            sem((3,)),
            sem((3,)),
            sem((3,)),
            sem((32,)),
            sem((32,)),
        ],
        compiler_params=pltpu.CompilerParams(
            collective_id=1, has_side_effects=True, vmem_limit_bytes=63 * 2**20
        ),
        cost_estimate=pl.CostEstimate(
            flops=34 * 10**9, bytes_accessed=40 * 10**6, transcendentals=20 * 10**6
        ),
    )(inv, tokens, meta, cotangent, master, momentum, variance)


def per_device(
    tokens,
    token_counts,
    segment_ids,
    dest_device,
    dest_slot,
    cotangent,
    master_weight,
    momentum,
    variance,
):
    position = lax.broadcasted_iota(jnp.int32, segment_ids.shape, 1)
    living = position < token_counts[:, None]
    matched = (segment_ids[:, :, None] == segment_ids[:, None, :]) & living[:, None, :]
    lengths = jnp.where(living, jnp.sum(matched, axis=2, dtype=jnp.int32), 0).reshape(16, 128)
    peers = jnp.arange(32, dtype=jnp.int32)
    chosen = dest_device[None, :] == peers[:, None]
    inv = jnp.sum(jnp.where(chosen, jnp.arange(16, dtype=jnp.int32)[None, :], 0), axis=1)
    slots = jnp.sum(jnp.where(chosen, dest_slot[None, :], 0), axis=1)
    lens = jnp.sum(jnp.where(chosen[:, :, None], lengths[None], 0), axis=1)
    row = lax.broadcasted_iota(jnp.int32, (32, 8, 128), 1)
    meta = jnp.where(row == 0, lens[:, None, :], slots[:, None, None])
    new_w, new_m, step = run(
        inv,
        tokens.reshape(16, 128, 1024),
        meta,
        cotangent.reshape(16, 128, 2048),
        master_weight,
        momentum,
        variance,
    )
    return (new_w.reshape(1024, 2048), new_m, step)


def solution(mesh):
    return jax.shard_map(
        per_device,
        mesh=mesh,
        in_specs=(
            P(("dp", "rep"), None, None),
            P(("dp", "rep")),
            P(("dp", "rep"), None),
            P(("dp", "rep")),
            P(("dp", "rep")),
            P(("dp", "rep"), None),
            P("dp", None),
            P(),
            P("dp", None),
        ),
        out_specs=(P(), P("dp", None), P("dp", None)),
        check_vma=False,
    )
```

time: 505 us -> 248 us (0.49)
  waiting for transfers between devices: 238 us -> 0 us
  Pallas kernels: 0 us -> 234 us
  blocking collectives: 65.4 us -> 0 us
  matrix products: 58.5 us -> 0 us
  starting transfers between devices: 44.4 us -> 0 us
  local copies, waits for them, and re-layouts: 51.5 us -> 7.17 us
  other arithmetic: 30.4 us -> 5.44 us
  between operations: 15.3 us -> 0.68 us
    pallas_call x0 -> x1, Pallas kernels: none -> 234 us  [run(): pl.pallas_call(kernel, out_shape=(jax.ShapeDtypeStruct((16, 2, 32, 2048),...]
    all_to_all x5 -> x0, waiting for transfers between devices: 154 us -> none  [the longest x1 102 us: per_device(): lax.all_to_all(send_blocks.reshape(data_peers, peer_room, block_tokens *...]
    psum x1 -> x0, blocking collectives: 65.4 us -> none  [per_device(): lax.psum((jnp.sum(master_weight * master_weight), jnp.sum(direction * dir...]
    dot_general x7 -> x0, matrix products: 58.5 us -> none  [the longest x1 18.7 us: per_device(): jnp.dot(local_tokens, lax.all_gather(master_weight.astype(jnp.bfloat16),...]
    all_gather x2 -> x0, waiting for transfers between devices: 44.4 us -> none  [the longest x1 44.4 us: per_device(): new_weights = lax.all_gather(fresh, 'dp', axis=0, tiled=True)]
    all_to_all x5 -> x0, starting transfers between devices: 44.1 us -> none  [the longest x1 14.2 us: per_device(): lax.all_to_all(sent_scale.reshape(data_peers, -1), 'dp', split_axis=0, co...]
    psum x1 -> x0, waiting for transfers between devices: 40 us -> none  [per_device(): lax.psum(partial_sum.astype(jnp.bfloat16), 'rep').astype(jnp.float32)]
    unnamed x11 -> x7, local copies, waits for them, and re-layouts: 39.2 us -> 6.26 us
  transfers between devices with their start and end apart: 8 -> 0, of which waited for: 5 -> 0; matrix products, arithmetic and copies ran while one was open for 18% -> 0% of each run, Pallas kernels for 0% -> 0%
where the time goes in v1:
time: 248 us
  Pallas kernels  234 us (94%)
  local copies, waits for them, and re-layouts  7.17 us (3%)
  other arithmetic  5.44 us (2%)
    pallas_call x1, Pallas kernels, run(): pl.pallas_call(kernel, out_shape=(jax.ShapeDtypeStruct((16, 2, 32, 2048),...  234 us
    unnamed x7, local copies, waits for them, and re-layouts  6.26 us

profile of v1, /device:TPU:1, one launch (start us, length us, event | category | flops | bytes accessed | tf_op | source)
XLA Modules:
  0.0 247.8 jit_solution(5702094742302706767)
XLA Ops:
  0.6 1.3 select_reduce_fusion.1
  1.9 0.7 iota_compare_fusion
  2.6 0.7 lt.24
  3.4 0.1 lt.25
  3.4 0.7 iota_compare_fusion.1
  4.2 0.1 copy.12
  4.3 1.7 convert_reduce_fusion
  6.0 0.1 compare_select_fusion
  6.1 0.2 select_reduce_fusion
  6.3 0.8 broadcast_select_fusion.meta
  7.0 234.5 %shard_map.112 = (bf16[16,2,32,2048]{3,2,1,0:T(8,128)(2,1)}, f32[32,2048]{1,0:T(8,128)}, f32[32,2048]{1,0:T(8,128)}) custom-call(s32[32]{0:T(128)} %get-tuple-element.10.inv, bf16[16,128,1024]{2,1,0:T(8,128)(2,1)} %bitcast.7, s32[32,8,128]{2,1,0:T(8,128)} %broadcast_select_fusion.meta, bf16[16,128,2048]{2,1,0:T(8,128)(2,1)} %bitcast.6, f32[32,2048]{1,0:T(8,128)} %master.1, ...), custom_call_target="tpu_custom_call" | custom-call | flops 33999998976 | bytes 40000000 | tf_op jit(solution)/shard_map/pallas_call | solution.py:379
  241.5 0.0 copy-start.1
  241.5 0.0 copy-start
  241.5 4.8 %copy.16 = bf16[1024,2048]{1,0:T(8,128)(2,1)} copy(bf16[1024,2048]{1,0:T(8,128)(2,1)} %bitcast.4) | data formatting | bytes 8388608
  246.4 0.0 copy-done.1
  246.4 0.7 copy.17
  247.1 0.0 copy-done
  247.1 0.7 copy.18
  (4 shorter events, 0.0 us)
Async XLA Ops:
  241.5 4.9 %copy-start.1 = (f32[32,2048]{1,0:T(8,128)S(1)}, f32[32,2048]{1,0:T(8,128)}, u32[]{:S(2)}) copy-start(f32[32,2048]{1,0:T(8,128)} %get-tuple-element.15) | copy-start | bytes 786436
  241.5 5.6 %copy-start = (f32[32,2048]{1,0:T(8,128)S(1)}, f32[32,2048]{1,0:T(8,128)}, u32[]{:S(2)}) copy-start(f32[32,2048]{1,0:T(8,128)} %get-tuple-element.16) | copy-start | bytes 786436

commit v2 on v1

v2 whole, which is shorter than its diff:
```python
import functools

import jax
import jax.numpy as jnp
from jax import lax
from jax.experimental import pallas as pl
from jax.experimental.pallas import tpu as pltpu
from jax.sharding import PartitionSpec as P

MESH = pl.DeviceIdType.MESH
F32 = jnp.float32
BF16 = jnp.bfloat16
momentum_decay = 0.9
learn_rate = 0.05
epsilon = 1e-06
normal_peak = 0.3989422804014327

GROUPS = (
    ((1, 1), (3, 3)),
    ((1, 3), (3, 1)),
    ((0, 2), (2, 0)),
    ((1, 2), (1, 0), (3, 2), (3, 0)),
    ((2, 1), (0, 1), (2, 3), (0, 3)),
    ((2, 2),),
)
MOVES = [(0, 0, 0), (0, 0, 1)]
for group in GROUPS:
    for core in (0, 1):
        for dy, dx in group:
            MOVES.append((dy, dx, core))

STEPS = ((20, 4), (24, 4), (28, 4), (30, 2), (32, 2))
EDGES = (0, 20, 24, 28, 30, 32)
WINDOW = 12
TILE = 512


def gelu_slope(a):
    u = jnp.abs(a)
    d = 1.0 + u * (0.3275911 * 0.7071067811865476)
    t = pl.reciprocal(d, approx=True)
    t = t * (2.0 - d * t)
    e = jnp.exp2((a * a) * (-0.5 * 1.4426950408889634))
    poly = t * (
        0.5 * 0.254829592
        + t
        * (
            0.5 * -0.284496736
            + t * (0.5 * 1.421413741 + t * (0.5 * -1.453152027 + t * (0.5 * 1.061405429)))
        )
    )
    h = e * (poly - normal_peak * u)
    return jnp.where(a >= 0.0, 1.0 - h, h)


def kernel(
    inv,
    tok_hbm,
    meta,
    cot_hbm,
    master,
    mom_hbm,
    variance,
    out_w,
    out_d,
    out_m,
    out_l,
    out_r,
    tok,
    stage,
    arr0,
    arr1,
    arr2,
    arr3,
    arr4,
    cot,
    w,
    acc,
    xs,
    xt,
    wt,
    metar,
    metas,
    orders,
    u,
    r1,
    s1,
    r2,
    s2,
    r3,
    r4,
    q,
    lsem,
    tss,
    tsr,
    mss,
    msr,
    gbs,
    gbr,
    gas,
    gar,
    gzs,
    gzr,
    gcs,
    gcr,
    c1s,
    c1r,
    c2s,
    c2r,
    c3s,
    c3r,
    c4s,
    c4r,
    qs,
    qr,
):
    me = lax.axis_index("dp")
    rep = lax.axis_index("rep")
    y = me // 8
    x = (me // 2) % 4
    c = me % 2
    a = (1 - c) * y + c * x
    b = (1 - c) * x + c * y
    sa = 4 * (1 - c) + c
    sb = 4 * c + (1 - c)
    arrs = (arr0, arr1, arr2, arr3, arr4)

    def place(ai, bi):
        return ai * sa + bi * sb

    def at_a(k):
        return (place((a + k) % 4, b) * 2 + c, rep)

    def at_b(k):
        return (place(a, (b + k) % 4) * 2 + c, rep)

    other = (y * 8 + x * 2 + 1 - c, rep)

    def copy(src, dst, ss, rs, dev):
        return pltpu.make_async_remote_copy(
            src_ref=src, dst_ref=dst, send_sem=ss, recv_sem=rs, device_id=dev, device_id_type=MESH
        )

    def peer(move):
        dy, dx, dc = move
        return (((y + dy) % 4) * 4 + (x + dx) % 4) * 2 + (c + dc) % 2

    def landing(j):
        n = max(i for i in range(5) if EDGES[i] <= j)
        return arrs[n].at[j - EDGES[n]]

    ctok = pltpu.make_async_copy(tok_hbm, tok, lsem.at[0])
    ccot = pltpu.make_async_copy(cot_hbm, cot, lsem.at[1])
    cmom = pltpu.make_async_copy(mom_hbm, acc, lsem.at[2])
    ctok.start()

    w[y * 4 + x, c] = master[...].astype(BF16)
    barrier = pltpu.get_barrier_semaphore()

    @pl.loop(1, 32)
    def _(k):
        pl.semaphore_signal(barrier, inc=1, device_id=((me + k) % 32, rep), device_id_type=MESH)

    for k in range(1, 4):
        pl.semaphore_signal(barrier, inc=1, device_id=(me, (rep + k) % 4), device_id_type=MESH)
    pl.semaphore_wait(barrier, 34)

    quarter = pl.ds(pl.multiple_of(rep * 512, 512), 512)
    gb = []
    for k in range(1, 4):
        part = w.at[y * 4 + x, c, :, quarter]
        gb.append(copy(part, part, gbs.at[0, k - 1], gbr.at[0, k - 1], at_b(k)))
        gb[-1].start()

    metacopies = []
    for j in range(1, 32):
        p = peer(MOVES[j])
        cp = copy(meta.at[p], metar.at[j], mss.at[j], msr.at[j], (p, rep))
        cp.start()
        metacopies.append(cp)
    metar[0] = meta[me]

    ctok.wait()
    ccot.start()
    cmom.start()
    sends = [None]
    arr0[0] = tok[inv[me]]
    ga = []
    gz = []
    gc = []
    for j in range(1, 32):
        if j > WINDOW:
            sends[j - WINDOW].wait_send()
        p = peer(MOVES[j])
        spot = stage.at[(j - 1) % WINDOW]
        spot[...] = tok[inv[p]]
        cp = copy(spot, landing(j), tss.at[j], tsr.at[j], (p, rep))
        cp.start()
        sends.append(cp)
        if j == 4:
            for cp in gb:
                cp.wait()
            for k in range(1, 4):
                for bb in range(4):
                    part = w.at[place(a, bb), c, :, quarter]
                    ga.append(copy(part, part, gas.at[0, k - 1, bb], gar.at[0, k - 1, bb], at_a(k)))
                    ga[-1].start()
        if j == 10:
            for cp in ga:
                cp.wait()
            for k in range(1, 4):
                part = w.at[:, c, :, quarter]
                gz.append(copy(part, part, gzs.at[k - 1], gzr.at[k - 1], (me, (rep + k) % 4)))
                gz[-1].start()
    for cp in metacopies:
        cp.wait()
    cmeta = pltpu.make_async_copy(metar, metas, lsem.at[3])
    cmeta.start()
    cmom.wait()

    @pl.loop(0, 32)
    def _(i):
        rows = pl.ds(pl.multiple_of(i * 32, 32), 32)
        acc[rows, :] = acc[rows, :] * (momentum_decay / (1.0 - momentum_decay))

    cmeta.wait()
    count = jnp.int32(0)
    for j in range(32):
        count = count + jnp.minimum(metas[j, 1, 0], 1)
        orders[16 + j] = count

    @pl.loop(0, 16)
    def _(k):
        found = jnp.int32(0)
        for j in range(32):
            found = found + jnp.where(orders[16 + j] <= k, 1, 0)
        orders[k] = found

    ccot.wait()
    for cp in gz:
        cp.wait()
    part = w.at[:, c]
    cp = copy(part, part, gcs.at[0, 0], gcr.at[0, 0], other)
    cp.start()
    cp.wait()
    cw = pltpu.make_async_copy(w, out_w, lsem.at[5])
    cw.start()

    done = 0
    arrived = 1
    for number, (needed, blocks) in enumerate(STEPS):
        while arrived < needed:
            sends[arrived].wait_recv()
            arrived += 1
        rowcount = blocks * 128
        slots = []
        for i in range(blocks):
            o = jnp.minimum(orders[done + i], 31)
            slots.append(jnp.maximum(metas[o, 1, 0] - 1, 0))
            block = arrs[0][jnp.minimum(o, EDGES[1] - 1)]
            for n in range(1, number + 1):
                at = jnp.clip(o - EDGES[n], 0, EDGES[n + 1] - EDGES[n] - 1)
                block = lax.select(o >= EDGES[n], arrs[n][at], block)
            xs[i * 128 : (i + 1) * 128, :] = block
            xt[:, i * 128 : (i + 1) * 128] = jnp.transpose(block)
            lens = metar[o][0:1, :]
            weight = jnp.where(lens > 0, 1.0 / jnp.maximum(lens, 1).astype(F32), 0.0)
            wt[i * 128 : (i + 1) * 128, :] = jnp.transpose(jnp.broadcast_to(weight, (128, 128)))
        done += blocks

        @pl.loop(0, 2048 // TILE)
        def _(n):
            cols = pl.ds(pl.multiple_of(n * TILE, TILE), TILE)
            pre = jnp.dot(
                xs[0:rowcount, :], w[:, :, :, cols].reshape(1024, TILE), preferred_element_type=F32
            )
            parts = []
            for i in range(blocks):
                rows = slice(i * 128, (i + 1) * 128)
                wide = jnp.concatenate([wt[rows, :]] * (TILE // 128), axis=1)
                ci = cot[slots[i], :, cols].astype(F32)
                parts.append((ci * gelu_slope(pre[rows]) * wide).astype(BF16))
            delta = jnp.concatenate(parts, axis=0)
            acc[:, cols] += jnp.dot(xt[:, 0:rowcount], delta, preferred_element_type=F32)

    cw.wait()
    for j in range(32 - WINDOW, 32):
        sends[j].wait_send()

    def squeezed(yx, core):
        rows = pl.ds(pl.multiple_of((yx * 2 + core) * 32, 32), 32)
        moment = acc[rows, :] * (1.0 - momentum_decay)
        scale = jnp.sum(jnp.abs(moment), axis=1, keepdims=True) * (1.0 / 2048)
        unit = jnp.tanh(moment * (1.0 / (scale + epsilon)))
        return scale.astype(BF16).astype(F32) * unit.astype(BF16).astype(F32)

    @pl.loop(0, 16)
    def _(i):
        yx = place((a + 1 + i // 4) % 4, i % 4)
        u[i] = squeezed(yx, 1 - c).astype(BF16)
        copy(u.at[i], r1.at[yx], c1s.at[i], c1r.at[yx], other).start()

    def add_core(k):
        @pl.loop(0, 4)
        def _(bb):
            yx = place((a + k) % 4, bb)
            copy(u.at[0], r1.at[yx], c1s.at[0], c1r.at[yx], other).wait_recv()
            s1[k, bb] = (squeezed(yx, c) + r1[yx].astype(F32)).astype(BF16)

    stage2 = []
    for k in (2, 1, 3, 0):
        add_core(k)
        if k:
            cp = copy(s1.at[k], r2.at[k - 1], c2s.at[k - 1], c2r.at[k - 1], at_a(k))
            cp.start()
            stage2.append(cp)
    for cp in stage2:
        cp.wait()

    def add_a(bi):
        total = s1[0, bi].astype(F32)
        for k in range(3):
            total = total + r2[k, bi].astype(F32)
        return total

    stage3 = []
    for k in (2, 1, 3):
        s2[k - 1] = add_a((b + k) % 4).astype(BF16)
        cp = copy(s2.at[k - 1], r3.at[k - 1], c3s.at[k - 1], c3r.at[k - 1], at_b(k))
        cp.start()
        stage3.append(cp)
    total = add_a(b)
    for cp in stage3:
        cp.wait()
    for k in range(3):
        total = total + r3[k].astype(F32)
    r4[rep] = total.astype(BF16)
    stage4 = []
    for k in (2, 1, 3):
        cp = copy(r4.at[rep], r4.at[rep], c4s.at[k - 1], c4r.at[k - 1], (me, (rep + k) % 4))
        cp.start()
        stage4.append(cp)
    for cp in stage4:
        cp.wait()
    average = (
        r4[0].astype(F32) + r4[1].astype(F32) + r4[2].astype(F32) + r4[3].astype(F32)
    ) * (1.0 / 128)
    scale = jnp.sum(jnp.abs(average), axis=1, keepdims=True) * (1.0 / 2048)
    moment = scale * jnp.tanh(average / (scale + epsilon))
    out_m[...] = moment
    direction = moment / (jnp.sqrt(variance[...]) + epsilon)
    w[y * 4 + x, c] = direction.astype(BF16)

    def group(ai, bi):
        return w.at[place(ai, bi), c]

    dcopies = []

    def to_a(bi):
        for k in (2, 1, 3):
            cp = copy(group(a, bi), group(a, bi), gas.at[1, k - 1, bi], gar.at[1, k - 1, bi], at_a(k))
            cp.start()
            dcopies.append(cp)

    def to_core(ai, bi):
        yx = place(ai, bi)
        copy(w.at[yx, c], w.at[yx, c], gcs.at[1, yx], gcr.at[1, yx], other).start()

    gb = {}
    for k in (2, 1, 3):
        gb[k] = copy(group(a, b), group(a, b), gbs.at[1, k - 1], gbr.at[1, k - 1], at_b(k))
        gb[k].start()
    to_a(b)

    def folded(v):
        line = jnp.sum(v, axis=0, keepdims=True)
        out = line[:, 0:128]
        for i in range(1, 16):
            out = out + line[:, i * 128 : (i + 1) * 128]
        return out

    q[me] = jnp.concatenate(
        [
            folded(master[...] * master[...]),
            folded(direction * direction),
            jnp.zeros((6, 128), F32),
        ],
        axis=0,
    )
    out_l[...] = direction
    scalars = []
    for j in range(1, 32):
        cp = copy(q.at[me], q.at[me], qs.at[j], qr.at[j], (peer(MOVES[j]), rep))
        cp.start()
        scalars.append(cp)

    to_core(a, b)
    for k in (1, 3, 2):
        gb[k].wait()
        to_a((b - k + 4) % 4)
        to_core(a, (b - k + 4) % 4)
    for cp in scalars:
        cp.wait()
    sums = jnp.sum(jnp.sum(q[...], axis=0), axis=1, keepdims=True)
    roots = jnp.sqrt(sums)
    ratio = roots[0:1, :] / (roots[1:2, :] + epsilon)
    out_l[...] = out_l[...] * ratio
    out_r[...] = jnp.broadcast_to(ratio, (8, 128))

    for k in (1, 3, 2):
        ai = (a - k + 4) % 4

        @pl.loop(0, 4)
        def _(i):
            bi = (b + i) % 4
            copy(group(ai, bi), group(ai, bi), gas.at[1, k - 1, bi], gar.at[1, k - 1, bi], at_a(k)).wait_recv()
            to_core(ai, bi)

    half = pltpu.make_async_copy(w.at[:, c], out_d.at[:, c], lsem.at[4])
    half.start()

    @pl.loop(0, 16)
    def _(i):
        theirs = w.at[i, 1 - c]
        copy(theirs, theirs, gcs.at[1, i], gcr.at[1, i], other).wait_recv()

    rest = pltpu.make_async_copy(w.at[:, 1 - c], out_d.at[:, 1 - c], lsem.at[6])
    rest.start()
    for cp in dcopies:
        cp.wait_send()

    @pl.loop(0, 16)
    def _(i):
        copy(w.at[i, c], w.at[i, c], gcs.at[1, i], gcr.at[1, i], other).wait_send()
        copy(u.at[i], r1.at[i], c1s.at[i], c1r.at[i], other).wait_send()

    half.wait()
    rest.wait()


def run(inv, tokens, meta, cotangent, master, momentum, variance):
    sem = pltpu.SemaphoreType.DMA
    vmem = pl.BlockSpec(memory_space=pltpu.VMEM)
    hbm = pl.BlockSpec(memory_space=pl.ANY)
    return pl.pallas_call(
        kernel,
        out_shape=(
            jax.ShapeDtypeStruct((16, 2, 32, 2048), BF16),
            jax.ShapeDtypeStruct((16, 2, 32, 2048), BF16),
            jax.ShapeDtypeStruct((32, 2048), F32),
            jax.ShapeDtypeStruct((32, 2048), F32),
            jax.ShapeDtypeStruct((8, 128), F32),
        ),
        in_specs=[
            pl.BlockSpec(memory_space=pltpu.SMEM),
            hbm,
            vmem,
            hbm,
            vmem,
            hbm,
            vmem,
        ],
        out_specs=(hbm, hbm, vmem, vmem, vmem),
        scratch_shapes=[
            pltpu.VMEM((16, 128, 1024), BF16),
            pltpu.VMEM((WINDOW, 128, 1024), BF16),
            pltpu.VMEM((20, 128, 1024), BF16),
            pltpu.VMEM((4, 128, 1024), BF16),
            pltpu.VMEM((4, 128, 1024), BF16),
            pltpu.VMEM((2, 128, 1024), BF16),
            pltpu.VMEM((2, 128, 1024), BF16),
            pltpu.VMEM((16, 128, 2048), BF16),
            pltpu.VMEM((16, 2, 32, 2048), BF16),
            pltpu.VMEM((1024, 2048), F32),
            pltpu.VMEM((512, 1024), BF16),
            pltpu.VMEM((1024, 512), BF16),
            pltpu.VMEM((512, 128), F32),
            pltpu.VMEM((32, 8, 128), jnp.int32),
            pltpu.SMEM((32, 8, 128), jnp.int32),
            pltpu.SMEM((48,), jnp.int32),
            pltpu.VMEM((16, 32, 2048), BF16),
            pltpu.VMEM((16, 32, 2048), BF16),
            pltpu.VMEM((4, 4, 32, 2048), BF16),
            pltpu.VMEM((3, 4, 32, 2048), BF16),
            pltpu.VMEM((3, 32, 2048), BF16),
            pltpu.VMEM((3, 32, 2048), BF16),
            pltpu.VMEM((4, 32, 2048), BF16),
            pltpu.VMEM((32, 8, 128), F32),
            sem((7,)),
            sem((32,)),
            sem((32,)),
            sem((32,)),
            sem((32,)),
            sem((2, 3)),
            sem((2, 3)),
            sem((2, 3, 4)),
            sem((2, 3, 4)),
            sem((3,)),
            sem((3,)),
            sem((2, 16)),
            sem((2, 16)),
            sem((16,)),
            sem((16,)),
            sem((3,)),
            sem((3,)),
            sem((3,)),
            sem((3,)),
            sem((3,)),
            sem((3,)),
            sem((32,)),
            sem((32,)),
        ],
        compiler_params=pltpu.CompilerParams(
            collective_id=1, has_side_effects=True, vmem_limit_bytes=63 * 2**20
        ),
        cost_estimate=pl.CostEstimate(
            flops=18 * 10**9, bytes_accessed=40 * 10**6, transcendentals=20 * 10**6
        ),
    )(inv, tokens, meta, cotangent, master, momentum, variance)


def per_device(
    tokens,
    token_counts,
    segment_ids,
    dest_device,
    dest_slot,
    cotangent,
    master_weight,
    momentum,
    variance,
):
    position = lax.broadcasted_iota(jnp.int32, segment_ids.shape, 1)
    living = position < token_counts[:, None]
    matched = (segment_ids[:, :, None] == segment_ids[:, None, :]) & living[:, None, :]
    lengths = jnp.where(living, jnp.sum(matched, axis=2, dtype=jnp.int32), 0).reshape(16, 128)
    peers = jnp.arange(32, dtype=jnp.int32)
    chosen = dest_device[None, :] == peers[:, None]
    inv = jnp.sum(jnp.where(chosen, jnp.arange(16, dtype=jnp.int32)[None, :], 0), axis=1)
    slots = jnp.sum(jnp.where(chosen, dest_slot[None, :] + 1, 0), axis=1)
    lens = jnp.sum(jnp.where(chosen[:, :, None], lengths[None], 0), axis=1)
    row = lax.broadcasted_iota(jnp.int32, (32, 8, 128), 1)
    meta = jnp.where(row == 0, lens[:, None, :], slots[:, None, None])
    old_w, direction, new_m, step, ratio = run(
        inv,
        tokens.reshape(16, 128, 1024),
        meta,
        cotangent.reshape(16, 128, 2048),
        master_weight,
        momentum,
        variance,
    )
    new_w = old_w.astype(F32) - (learn_rate * ratio[0, 0]) * direction.astype(F32)
    return (new_w.astype(BF16).reshape(1024, 2048), new_m, step)


def solution(mesh):
    return jax.shard_map(
        per_device,
        mesh=mesh,
        in_specs=(
            P(("dp", "rep"), None, None),
            P(("dp", "rep")),
            P(("dp", "rep"), None),
            P(("dp", "rep")),
            P(("dp", "rep")),
            P(("dp", "rep"), None),
            P("dp", None),
            P(),
            P("dp", None),
        ),
        out_specs=(P(), P("dp", None), P("dp", None)),
        check_vma=False,
    )
```

time: 248 us -> 213 us (0.86)
  Pallas kernels: 234 us -> 194 us
  other arithmetic: 5.44 us -> 14 us
  local copies, waits for them, and re-layouts: 7.17 us -> 3.52 us
    pallas_call x1, Pallas kernels: 234 us -> 194 us  [run(): pl.pallas_call(kernel, out_shape=(jax.ShapeDtypeStruct((16, 2, 32, 2048),...]
    convert_element_type x0 -> x1, other arithmetic: none -> 7.9 us  [per_device(): return (new_w.astype(BF16).reshape(1024, 2048), new_m, step)]
    unnamed x7 -> x6, local copies, waits for them, and re-layouts: 6.26 us -> 1.41 us
where the time goes in v2:
time: 213 us
  Pallas kernels  194 us (91%)
  other arithmetic  14 us (7%)
  local copies, waits for them, and re-layouts  3.52 us (2%)
    pallas_call x1, Pallas kernels, run(): pl.pallas_call(kernel, out_shape=(jax.ShapeDtypeStruct((16, 2, 32, 2048),...  194 us
    convert_element_type x1, other arithmetic, per_device(): return (new_w.astype(BF16).reshape(1024, 2048), new_m, step)  7.9 us

profile of v2, /device:TPU:1, one launch (start us, length us, event | category | flops | bytes accessed | tf_op | source)
XLA Modules:
  0.0 212.7 jit_solution(7501624248592399447)
XLA Ops:
  0.6 0.7 broadcast_add_fusion
  1.3 1.2 select_reduce_fusion.1
  2.5 0.7 iota_compare_fusion
  3.3 0.7 lt.24
  4.0 0.1 lt.25
  4.1 0.7 iota_compare_fusion.1
  4.8 0.1 copy.12
  4.9 1.7 convert_reduce_fusion
  6.7 0.1 compare_select_fusion
  6.7 0.2 select_reduce_fusion
  6.9 0.8 broadcast_select_fusion.meta
  7.6 193.8 %shard_map.112 = (bf16[16,2,32,2048]{3,2,1,0:T(8,128)(2,1)}, bf16[16,2,32,2048]{3,2,1,0:T(8,128)(2,1)}, f32[32,2048]{1,0:T(8,128)}, f32[32,2048]{1,0:T(8,128)}, f32[8,128]{1,0:T(8,128)}) custom-call(s32[32]{0:T(128)} %get-tuple-element.14.inv, bf16[16,128,1024]{2,1,0:T(8,128)(2,1)} %bitcast.8, s32[32,8,128]{2,1,0:T(8,128)} %broadcast_select_fusion.meta, ...), custom_call_target="tpu_custom_call" | custom-call | flops 17999998976 | bytes 40000000 | tf_op jit(solution)/shard_map/pallas_call | solution.py:445
  201.5 1.2 slice.3
  203.3 0.0 copy-start.1
  203.3 0.0 copy-start
  203.3 7.9 %subtract_convert_fusion = bf16[16,2,32,2048]{3,2,1,0:T(8,128)(2,1)} fusion(bf16[16,2,32,2048]{3,2,1,0:T(8,128)(2,1)} %get-tuple-element.10, bf16[16,2,32,2048]{3,2,1,0:T(8,128)(2,1)} %get-tuple-element.8, f32[]{:T(128)} %bitcast.3), kind=kLoop, calls=%fused_computation | loop fusion | flops 10485760 | bytes 12582916 | tf_op jit(solution)/shard_map/convert_element_type | solution.py:554
  211.2 0.0 copy-done.1
  211.2 0.7 copy.15
  211.9 0.0 copy-done
  211.9 0.7 copy.16
  (4 shorter events, 0.0 us)
Async XLA Ops:
  203.3 7.9 %copy-start.1 = (f32[32,2048]{1,0:T(8,128)S(1)}, f32[32,2048]{1,0:T(8,128)}, u32[]{:S(2)}) copy-start(f32[32,2048]{1,0:T(8,128)} %get-tuple-element.19) | copy-start | bytes 786436
  203.3 8.6 %copy-start = (f32[32,2048]{1,0:T(8,128)S(1)}, f32[32,2048]{1,0:T(8,128)}, u32[]{:S(2)}) copy-start(f32[32,2048]{1,0:T(8,128)} %get-tuple-element.20) | copy-start | bytes 786436

commit v3 on v2

--- a/solution.py
+++ b/solution.py
@@ -17,10 +17,12 @@
 
 GROUPS = (
     ((1, 1), (3, 3)),
+    ((1, 2), (3, 0)),
+    ((2, 1), (0, 3)),
     ((1, 3), (3, 1)),
+    ((3, 2), (1, 0)),
+    ((2, 3), (0, 1)),
     ((0, 2), (2, 0)),
-    ((1, 2), (1, 0), (3, 2), (3, 0)),
-    ((2, 1), (0, 1), (2, 3), (0, 3)),
     ((2, 2),),
 )
 MOVES = [(0, 0, 0), (0, 0, 1)]
@@ -29,10 +31,10 @@
         for dy, dx in group:
             MOVES.append((dy, dx, core))
 
-STEPS = ((20, 4), (24, 4), (28, 4), (30, 2), (32, 2))
-EDGES = (0, 20, 24, 28, 30, 32)
-WINDOW = 12
-TILE = 512
+EDGES = (0, 18, 20, 22, 24, 26, 28, 30, 32)
+BUFFERS = len(EDGES) - 1
+WINDOW = 16
+TILE = 1024
 
 
 def gelu_slope(a):
@@ -54,18 +56,18 @@
 
 
 def kernel(
-    inv,
+    counts,
+    dest,
+    dslot,
+    segments,
     tok_hbm,
-    meta,
     cot_hbm,
     master,
     mom_hbm,
     variance,
     out_w,
-    out_d,
     out_m,
     out_l,
-    out_r,
     tok,
     stage,
     arr0,
@@ -73,8 +75,12 @@
     arr2,
     arr3,
     arr4,
+    arr5,
+    arr6,
+    arr7,
     cot,
     w,
+    gathered,
     acc,
     xs,
     xt,
@@ -82,6 +88,9 @@
     metar,
     metas,
     orders,
+    table,
+    lengths,
+    metasent,
     u,
     r1,
     s1,
@@ -91,6 +100,7 @@
     r4,
     q,
     lsem,
+    outsem,
     tss,
     tsr,
     mss,
@@ -123,7 +133,7 @@
     b = (1 - c) * x + c * y
     sa = 4 * (1 - c) + c
     sb = 4 * c + (1 - c)
-    arrs = (arr0, arr1, arr2, arr3, arr4)
+    arrs = (arr0, arr1, arr2, arr3, arr4, arr5, arr6, arr7)
 
     def place(ai, bi):
         return ai * sa + bi * sb
@@ -146,7 +156,7 @@
         return (((y + dy) % 4) * 4 + (x + dx) % 4) * 2 + (c + dc) % 2
 
     def landing(j):
-        n = max(i for i in range(5) if EDGES[i] <= j)
+        n = max(i for i in range(BUFFERS) if EDGES[i] <= j)
         return arrs[n].at[j - EDGES[n]]
 
     ctok = pltpu.make_async_copy(tok_hbm, tok, lsem.at[0])
@@ -163,6 +173,19 @@
 
     for k in range(1, 4):
         pl.semaphore_signal(barrier, inc=1, device_id=(me, (rep + k) % 4), device_id_type=MESH)
+
+    @pl.loop(0, 32)
+    def _(p):
+        block, there, slot = jnp.int32(0), jnp.int32(0), jnp.int32(0)
+        for i in range(16):
+            same = jnp.where(dest[i] == p, 1, 0)
+            block = block + same * i
+            there = there + same
+            slot = slot + same * (dslot[i] + 1)
+        table[p] = jnp.minimum(block, 15)
+        table[32 + p] = there
+        table[64 + p] = slot
+
     pl.semaphore_wait(barrier, 34)
 
     quarter = pl.ds(pl.multiple_of(rep * 512, 512), 512)
@@ -172,19 +195,12 @@
         gb.append(copy(part, part, gbs.at[0, k - 1], gbr.at[0, k - 1], at_b(k)))
         gb[-1].start()
 
-    metacopies = []
-    for j in range(1, 32):
-        p = peer(MOVES[j])
-        cp = copy(meta.at[p], metar.at[j], mss.at[j], msr.at[j], (p, rep))
-        cp.start()
-        metacopies.append(cp)
-    metar[0] = meta[me]
-
     ctok.wait()
     ccot.start()
     cmom.start()
     sends = [None]
-    arr0[0] = tok[inv[me]]
+    arr0[0] = tok[table[me]]
+    metacopies = []
     ga = []
     gz = []
     gc = []
@@ -193,7 +209,7 @@
             sends[j - WINDOW].wait_send()
         p = peer(MOVES[j])
         spot = stage.at[(j - 1) % WINDOW]
-        spot[...] = tok[inv[p]]
+        spot[...] = tok[table[p]]
         cp = copy(spot, landing(j), tss.at[j], tsr.at[j], (p, rep))
         cp.start()
         sends.append(cp)
@@ -205,6 +221,31 @@
                     part = w.at[place(a, bb), c, :, quarter]
                     ga.append(copy(part, part, gas.at[0, k - 1, bb], gar.at[0, k - 1, bb], at_a(k)))
                     ga[-1].start()
+        if j == 6:
+            for r in range(4):
+                ids = segments[r : r + 1, :]
+                live = lax.broadcasted_iota(jnp.int32, (1, 512), 1) < counts[r]
+                found = jnp.zeros((1, 512), jnp.int32)
+                for v in range(8):
+                    hit = jnp.where((ids == v) & live, 1, 0)
+                    found = found + hit * jnp.sum(hit, axis=1, keepdims=True)
+                for i in range(4):
+                    lengths[r * 4 + i] = jnp.broadcast_to(
+                        found[:, i * 128 : (i + 1) * 128], (8, 128)
+                    )
+            line = lax.broadcasted_iota(jnp.int32, (8, 128), 0)
+            for n in range(32):
+                p = peer(MOVES[n])
+                lens = lengths[table[p]] * table[32 + p]
+                value = jnp.where(line == 0, lens, table[64 + p])
+                if n == 0:
+                    metar[0] = value
+                else:
+                    metasent[n] = value
+                    metacopies.append(
+                        copy(metasent.at[n], metar.at[n], mss.at[n], msr.at[n], (p, rep))
+                    )
+                    metacopies[-1].start()
         if j == 10:
             for cp in ga:
                 cp.wait()
@@ -243,12 +284,11 @@
     cp = copy(part, part, gcs.at[0, 0], gcr.at[0, 0], other)
     cp.start()
     cp.wait()
-    cw = pltpu.make_async_copy(w, out_w, lsem.at[5])
-    cw.start()
-
     done = 0
     arrived = 1
-    for number, (needed, blocks) in enumerate(STEPS):
+    blocks = 2
+    for number in range(BUFFERS):
+        needed = EDGES[number + 1]
         while arrived < needed:
             sends[arrived].wait_recv()
             arrived += 1
@@ -256,7 +296,7 @@
         slots = []
         for i in range(blocks):
             o = jnp.minimum(orders[done + i], 31)
-            slots.append(jnp.maximum(metas[o, 1, 0] - 1, 0))
+            slots.append(jnp.clip(metas[o, 1, 0] - 1, 0, 15))
             block = arrs[0][jnp.minimum(o, EDGES[1] - 1)]
             for n in range(1, number + 1):
                 at = jnp.clip(o - EDGES[n], 0, EDGES[n + 1] - EDGES[n] - 1)
@@ -283,7 +323,6 @@
             delta = jnp.concatenate(parts, axis=0)
             acc[:, cols] += jnp.dot(xt[:, 0:rowcount], delta, preferred_element_type=F32)
 
-    cw.wait()
     for j in range(32 - WINDOW, 32):
         sends[j].wait_send()
 
@@ -349,10 +388,10 @@
     moment = scale * jnp.tanh(average / (scale + epsilon))
     out_m[...] = moment
     direction = moment / (jnp.sqrt(variance[...]) + epsilon)
-    w[y * 4 + x, c] = direction.astype(BF16)
+    gathered[y * 4 + x, c] = direction.astype(BF16)
 
     def group(ai, bi):
-        return w.at[place(ai, bi), c]
+        return gathered.at[place(ai, bi), c]
 
     dcopies = []
 
@@ -364,7 +403,7 @@
 
     def to_core(ai, bi):
         yx = place(ai, bi)
-        copy(w.at[yx, c], w.at[yx, c], gcs.at[1, yx], gcr.at[1, yx], other).start()
+        copy(gathered.at[yx, c], gathered.at[yx, c], gcs.at[1, yx], gcr.at[1, yx], other).start()
 
     gb = {}
     for k in (2, 1, 3):
@@ -405,7 +444,17 @@
     roots = jnp.sqrt(sums)
     ratio = roots[0:1, :] / (roots[1:2, :] + epsilon)
     out_l[...] = out_l[...] * ratio
-    out_r[...] = jnp.broadcast_to(ratio, (8, 128))
+    factor = learn_rate * ratio
+
+    def update(yx, core):
+        new = w[yx, core].astype(F32) - factor * gathered[yx, core].astype(F32)
+        w[yx, core] = new.astype(BF16)
+        at = yx * 2 + core
+        pltpu.make_async_copy(w.at[yx, core], out_w.at[yx, core], outsem.at[at]).start()
+
+    @pl.loop(0, 4)
+    def _(i):
+        update(place(a, i), c)
 
     for k in (1, 3, 2):
         ai = (a - k + 4) % 4
@@ -413,71 +462,80 @@
         @pl.loop(0, 4)
         def _(i):
             bi = (b + i) % 4
-            copy(group(ai, bi), group(ai, bi), gas.at[1, k - 1, bi], gar.at[1, k - 1, bi], at_a(k)).wait_recv()
+            copy(
+                group(ai, bi), group(ai, bi), gas.at[1, k - 1, bi], gar.at[1, k - 1, bi], at_a(k)
+            ).wait_recv()
             to_core(ai, bi)
-
-    half = pltpu.make_async_copy(w.at[:, c], out_d.at[:, c], lsem.at[4])
-    half.start()
+            update(place(ai, bi), c)
 
     @pl.loop(0, 16)
     def _(i):
-        theirs = w.at[i, 1 - c]
+        theirs = gathered.at[i, 1 - c]
         copy(theirs, theirs, gcs.at[1, i], gcr.at[1, i], other).wait_recv()
-
-    rest = pltpu.make_async_copy(w.at[:, 1 - c], out_d.at[:, 1 - c], lsem.at[6])
-    rest.start()
+        update(i, 1 - c)
+
     for cp in dcopies:
         cp.wait_send()
 
     @pl.loop(0, 16)
     def _(i):
-        copy(w.at[i, c], w.at[i, c], gcs.at[1, i], gcr.at[1, i], other).wait_send()
+        mine = gathered.at[i, c]
+        copy(mine, mine, gcs.at[1, i], gcr.at[1, i], other).wait_send()
         copy(u.at[i], r1.at[i], c1s.at[i], c1r.at[i], other).wait_send()
-
-    half.wait()
-    rest.wait()
-
-
-def run(inv, tokens, meta, cotangent, master, momentum, variance):
+        for core in range(2):
+            pltpu.make_async_copy(
+                w.at[i, core], out_w.at[i, core], outsem.at[i * 2 + core]
+            ).wait()
+
+
+def run(counts, dest, dslot, segments, tokens, cotangent, master, momentum, variance):
     sem = pltpu.SemaphoreType.DMA
     vmem = pl.BlockSpec(memory_space=pltpu.VMEM)
+    smem = pl.BlockSpec(memory_space=pltpu.SMEM)
     hbm = pl.BlockSpec(memory_space=pl.ANY)
     return pl.pallas_call(
         kernel,
         out_shape=(
             jax.ShapeDtypeStruct((16, 2, 32, 2048), BF16),
-            jax.ShapeDtypeStruct((16, 2, 32, 2048), BF16),
             jax.ShapeDtypeStruct((32, 2048), F32),
             jax.ShapeDtypeStruct((32, 2048), F32),
-            jax.ShapeDtypeStruct((8, 128), F32),
         ),
         in_specs=[
-            pl.BlockSpec(memory_space=pltpu.SMEM),
+            smem,
+            smem,
+            smem,
+            vmem,
             hbm,
-            vmem,
             hbm,
             vmem,
             hbm,
             vmem,
         ],
-        out_specs=(hbm, hbm, vmem, vmem, vmem),
+        out_specs=(hbm, vmem, vmem),
         scratch_shapes=[
             pltpu.VMEM((16, 128, 1024), BF16),
             pltpu.VMEM((WINDOW, 128, 1024), BF16),
-            pltpu.VMEM((20, 128, 1024), BF16),
-            pltpu.VMEM((4, 128, 1024), BF16),
-            pltpu.VMEM((4, 128, 1024), BF16),
+            pltpu.VMEM((18, 128, 1024), BF16),
+            pltpu.VMEM((2, 128, 1024), BF16),
+            pltpu.VMEM((2, 128, 1024), BF16),
+            pltpu.VMEM((2, 128, 1024), BF16),
+            pltpu.VMEM((2, 128, 1024), BF16),
+            pltpu.VMEM((2, 128, 1024), BF16),
             pltpu.VMEM((2, 128, 1024), BF16),
             pltpu.VMEM((2, 128, 1024), BF16),
             pltpu.VMEM((16, 128, 2048), BF16),
             pltpu.VMEM((16, 2, 32, 2048), BF16),
+            pltpu.VMEM((16, 2, 32, 2048), BF16),
             pltpu.VMEM((1024, 2048), F32),
-            pltpu.VMEM((512, 1024), BF16),
-            pltpu.VMEM((1024, 512), BF16),
-            pltpu.VMEM((512, 128), F32),
+            pltpu.VMEM((256, 1024), BF16),
+            pltpu.VMEM((1024, 256), BF16),
+            pltpu.VMEM((256, 128), F32),
             pltpu.VMEM((32, 8, 128), jnp.int32),
             pltpu.SMEM((32, 8, 128), jnp.int32),
             pltpu.SMEM((48,), jnp.int32),
+            pltpu.SMEM((96,), jnp.int32),
+            pltpu.VMEM((16, 8, 128), jnp.int32),
+            pltpu.VMEM((32, 8, 128), jnp.int32),
             pltpu.VMEM((16, 32, 2048), BF16),
             pltpu.VMEM((16, 32, 2048), BF16),
             pltpu.VMEM((4, 4, 32, 2048), BF16),
@@ -486,7 +544,8 @@
             pltpu.VMEM((3, 32, 2048), BF16),
             pltpu.VMEM((4, 32, 2048), BF16),
             pltpu.VMEM((32, 8, 128), F32),
-            sem((7,)),
+            sem((4,)),
+            sem((32,)),
             sem((32,)),
             sem((32,)),
             sem((32,)),
@@ -516,7 +575,13 @@
         cost_estimate=pl.CostEstimate(
             flops=18 * 10**9, bytes_accessed=40 * 10**6, transcendentals=20 * 10**6
         ),
-    )(inv, tokens, meta, cotangent, master, momentum, variance)
+    )(counts, dest, dslot, segments, tokens, cotangent, master, momentum, variance)
+
+
+def settle(w_in, m_in, l_in, w_out, m_out, l_out):
+    w_out[...] = w_in[...]
+    m_out[...] = m_in[...]
+    l_out[...] = l_in[...]
 
 
 def per_device(
@@ -530,28 +595,30 @@
     momentum,
     variance,
 ):
-    position = lax.broadcasted_iota(jnp.int32, segment_ids.shape, 1)
-    living = position < token_counts[:, None]
-    matched = (segment_ids[:, :, None] == segment_ids[:, None, :]) & living[:, None, :]
-    lengths = jnp.where(living, jnp.sum(matched, axis=2, dtype=jnp.int32), 0).reshape(16, 128)
-    peers = jnp.arange(32, dtype=jnp.int32)
-    chosen = dest_device[None, :] == peers[:, None]
-    inv = jnp.sum(jnp.where(chosen, jnp.arange(16, dtype=jnp.int32)[None, :], 0), axis=1)
-    slots = jnp.sum(jnp.where(chosen, dest_slot[None, :] + 1, 0), axis=1)
-    lens = jnp.sum(jnp.where(chosen[:, :, None], lengths[None], 0), axis=1)
-    row = lax.broadcasted_iota(jnp.int32, (32, 8, 128), 1)
-    meta = jnp.where(row == 0, lens[:, None, :], slots[:, None, None])
-    old_w, direction, new_m, step, ratio = run(
-        inv,
+    new_w, new_m, step = run(
+        token_counts,
+        dest_device,
+        dest_slot,
+        segment_ids,
         tokens.reshape(16, 128, 1024),
-        meta,
         cotangent.reshape(16, 128, 2048),
         master_weight,
         momentum,
         variance,
     )
-    new_w = old_w.astype(F32) - (learn_rate * ratio[0, 0]) * direction.astype(F32)
-    return (new_w.astype(BF16).reshape(1024, 2048), new_m, step)
+    specs = [pl.BlockSpec((rows, 2048), lambda i: (i, 0)) for rows in (256, 8, 8)]
+    return pl.pallas_call(
+        settle,
+        grid=(4,),
+        out_shape=(
+            jax.ShapeDtypeStruct((1024, 2048), BF16),
+            jax.ShapeDtypeStruct((32, 2048), F32),
+            jax.ShapeDtypeStruct((32, 2048), F32),
+        ),
+        in_specs=specs,
+        out_specs=tuple(specs),
+        cost_estimate=pl.CostEstimate(flops=0, bytes_accessed=9 * 10**6, transcendentals=0),
+    )(new_w.reshape(1024, 2048), new_m, step)
 
 
 def solution(mesh):

time: 213 us -> 207 us (0.972)
  other arithmetic: 14 us -> 0 us
  Pallas kernels: 194 us -> 205 us
  local copies, waits for them, and re-layouts: 3.52 us -> 0 us
    convert_element_type x1 -> x0, other arithmetic: 7.9 us -> none  [per_device(): return (new_w.astype(BF16).reshape(1024, 2048), new_m, step)]
    pallas_call x1, Pallas kernels: 194 us -> 200 us  [run(): pl.pallas_call(kernel, out_shape=(jax.ShapeDtypeStruct((16, 2, 32, 2048),...]
    pallas_call x0 -> x1, Pallas kernels: none -> 4.96 us  [per_device(): pl.pallas_call(settle, grid=(4,), out_shape=(jax.ShapeDtypeStruct((1024,...]
    reduce_sum x3 -> x0, other arithmetic: 3.12 us -> none  [the longest x1 1.72 us: per_device(): jnp.sum(matched, axis=2, dtype=jnp.int32)]
where the time goes in v3:
time: 207 us; the launch traced here: 206 us
  Pallas kernels  205 us (99%)
    pallas_call x1, Pallas kernels, run(): pl.pallas_call(kernel, out_shape=(jax.ShapeDtypeStruct((16, 2, 32, 2048),...  200 us
    pallas_call x1, Pallas kernels, per_device(): pl.pallas_call(settle, grid=(4,), out_shape=(jax.ShapeDtypeStruct((1024,...  4.96 us

profile of v3, /device:TPU:1, one launch (start us, length us, event | category | flops | bytes accessed | tf_op | source)
XLA Modules:
  0.0 205.6 jit_solution(12460561790667626550)
XLA Ops:
  0.6 200.0 %shard_map.112 = (bf16[16,2,32,2048]{3,2,1,0:T(8,128)(2,1)}, f32[32,2048]{1,0:T(8,128)}, f32[32,2048]{1,0:T(8,128)}) custom-call(s32[4]{0:T(128)} %counts.1, s32[16]{0:T(128)} %dest.1, s32[16]{0:T(128)} %dslot.1, s32[4,512]{1,0:T(4,128)} %segments.1, bf16[16,128,1024]{2,1,0:T(8,128)(2,1)} %bitcast.5, bf16[16,128,2048]{2,1,0:T(8,128)(2,1)} %bitcast.4, ...), custom_call_target="tpu_custom_call" | custom-call | flops 17999998976 | bytes 40000000 | tf_op jit(solution)/shard_map/pallas_call | solution.py:496
  200.6 5.0 %shard_map.113 = (bf16[1024,2048]{1,0:T(8,128)(2,1)}, f32[32,2048]{1,0:T(8,128)}, f32[32,2048]{1,0:T(8,128)}) custom-call(bf16[1024,2048]{1,0:T(8,128)(2,1)} %bitcast.3, f32[32,2048]{1,0:T(8,128)} %get-tuple-element.7.m_in, f32[32,2048]{1,0:T(8,128)} %get-tuple-element.8.l_in), custom_call_target="tpu_custom_call" | custom-call | bytes 9000000 | tf_op jit(solution)/shard_map/pallas_call | solution.py:610

commit v4 on v3

--- a/solution.py
+++ b/solution.py
@@ -33,7 +33,8 @@
 
 EDGES = (0, 18, 20, 22, 24, 26, 28, 30, 32)
 BUFFERS = len(EDGES) - 1
-WINDOW = 16
+WINDOW = 8
+AHEAD = 6
 TILE = 1024
 
 
@@ -204,7 +205,8 @@
     ga = []
     gz = []
     gc = []
-    for j in range(1, 32):
+
+    def send(j):
         if j > WINDOW:
             sends[j - WINDOW].wait_send()
         p = peer(MOVES[j])
@@ -213,6 +215,9 @@
         cp = copy(spot, landing(j), tss.at[j], tsr.at[j], (p, rep))
         cp.start()
         sends.append(cp)
+
+    for j in range(1, EDGES[1] + AHEAD):
+        send(j)
         if j == 4:
             for cp in gb:
                 cp.wait()
@@ -289,6 +294,8 @@
     blocks = 2
     for number in range(BUFFERS):
         needed = EDGES[number + 1]
+        while len(sends) < min(needed + AHEAD, 32):
+            send(len(sends))
         while arrived < needed:
             sends[arrived].wait_recv()
             arrived += 1

time: 207 us -> 195 us (0.942)
  Pallas kernels: 205 us -> 194 us
    pallas_call x1, Pallas kernels: 200 us -> 189 us  [run(): pl.pallas_call(kernel, out_shape=(jax.ShapeDtypeStruct((16, 2, 32, 2048),...]
where the time goes in v4:
time: 195 us; the launch traced here: 194 us
  Pallas kernels  194 us (99%)
    pallas_call x1, Pallas kernels, run(): pl.pallas_call(kernel, out_shape=(jax.ShapeDtypeStruct((16, 2, 32, 2048),...  189 us
    pallas_call x1, Pallas kernels, per_device(): pl.pallas_call(settle, grid=(4,), out_shape=(jax.ShapeDtypeStruct((1024,...  4.96 us

profile of v4, /device:TPU:1, one launch (start us, length us, event | category | flops | bytes accessed | tf_op | source)
XLA Modules:
  0.0 194.5 jit_solution(16982260369265620782)
XLA Ops:
  0.6 188.9 %shard_map.112 = (bf16[16,2,32,2048]{3,2,1,0:T(8,128)(2,1)}, f32[32,2048]{1,0:T(8,128)}, f32[32,2048]{1,0:T(8,128)}) custom-call(s32[4]{0:T(128)} %counts.1, s32[16]{0:T(128)} %dest.1, s32[16]{0:T(128)} %dslot.1, s32[4,512]{1,0:T(4,128)} %segments.1, bf16[16,128,1024]{2,1,0:T(8,128)(2,1)} %bitcast.5, bf16[16,128,2048]{2,1,0:T(8,128)(2,1)} %bitcast.4, ...), custom_call_target="tpu_custom_call" | custom-call | flops 17999998976 | bytes 40000000 | tf_op jit(solution)/shard_map/pallas_call | solution.py:503
  189.5 5.0 %shard_map.113 = (bf16[1024,2048]{1,0:T(8,128)(2,1)}, f32[32,2048]{1,0:T(8,128)}, f32[32,2048]{1,0:T(8,128)}) custom-call(bf16[1024,2048]{1,0:T(8,128)(2,1)} %bitcast.3, f32[32,2048]{1,0:T(8,128)} %get-tuple-element.7.m_in, f32[32,2048]{1,0:T(8,128)} %get-tuple-element.8.l_in), custom_call_target="tpu_custom_call" | custom-call | bytes 9000000 | tf_op jit(solution)/shard_map/pallas_call | solution.py:617

commit v5 on v4

--- a/solution.py
+++ b/solution.py
@@ -31,10 +31,10 @@
         for dy, dx in group:
             MOVES.append((dy, dx, core))
 
-EDGES = (0, 18, 20, 22, 24, 26, 28, 30, 32)
+EDGES = (0, 18, 22, 26, 30, 32)
 BUFFERS = len(EDGES) - 1
 WINDOW = 8
-AHEAD = 6
+AHEAD = 8
 TILE = 1024
 
 
@@ -76,9 +76,6 @@
     arr2,
     arr3,
     arr4,
-    arr5,
-    arr6,
-    arr7,
     cot,
     w,
     gathered,
@@ -134,7 +131,7 @@
     b = (1 - c) * x + c * y
     sa = 4 * (1 - c) + c
     sb = 4 * c + (1 - c)
-    arrs = (arr0, arr1, arr2, arr3, arr4, arr5, arr6, arr7)
+    arrs = (arr0, arr1, arr2, arr3, arr4)
 
     def place(ai, bi):
         return ai * sa + bi * sb
@@ -215,6 +212,37 @@
         cp = copy(spot, landing(j), tss.at[j], tsr.at[j], (p, rep))
         cp.start()
         sends.append(cp)
+
+    def prepare():
+        for cp in metacopies:
+            cp.wait()
+        cmeta = pltpu.make_async_copy(metar, metas, lsem.at[3])
+        cmeta.start()
+        cmom.wait()
+
+        @pl.loop(0, 32)
+        def _(i):
+            rows = pl.ds(pl.multiple_of(i * 32, 32), 32)
+            acc[rows, :] = acc[rows, :] * (momentum_decay / (1.0 - momentum_decay))
+
+        cmeta.wait()
+        count = jnp.int32(0)
+        for j in range(32):
+            count = count + jnp.minimum(metas[j, 1, 0], 1)
+            orders[16 + j] = count
+
+        @pl.loop(0, 16)
+        def _(k):
+            found = jnp.int32(0)
+            for j in range(32):
+                found = found + jnp.where(orders[16 + j] <= k, 1, 0)
+            orders[k] = found
+
+        for cp in gz:
+            cp.wait()
+        part = w.at[:, c]
+        gc.append(copy(part, part, gcs.at[0, 0], gcr.at[0, 0], other))
+        gc[0].start()
 
     for j in range(1, EDGES[1] + AHEAD):
         send(j)
@@ -258,40 +286,13 @@
                 part = w.at[:, c, :, quarter]
                 gz.append(copy(part, part, gzs.at[k - 1], gzr.at[k - 1], (me, (rep + k) % 4)))
                 gz[-1].start()
-    for cp in metacopies:
-        cp.wait()
-    cmeta = pltpu.make_async_copy(metar, metas, lsem.at[3])
-    cmeta.start()
-    cmom.wait()
-
-    @pl.loop(0, 32)
-    def _(i):
-        rows = pl.ds(pl.multiple_of(i * 32, 32), 32)
-        acc[rows, :] = acc[rows, :] * (momentum_decay / (1.0 - momentum_decay))
-
-    cmeta.wait()
-    count = jnp.int32(0)
-    for j in range(32):
-        count = count + jnp.minimum(metas[j, 1, 0], 1)
-        orders[16 + j] = count
-
-    @pl.loop(0, 16)
-    def _(k):
-        found = jnp.int32(0)
-        for j in range(32):
-            found = found + jnp.where(orders[16 + j] <= k, 1, 0)
-        orders[k] = found
-
+        if j == 17:
+            prepare()
     ccot.wait()
-    for cp in gz:
-        cp.wait()
-    part = w.at[:, c]
-    cp = copy(part, part, gcs.at[0, 0], gcr.at[0, 0], other)
-    cp.start()
-    cp.wait()
+    gc[0].wait()
+
     done = 0
     arrived = 1
-    blocks = 2
     for number in range(BUFFERS):
         needed = EDGES[number + 1]
         while len(sends) < min(needed + AHEAD, 32):
@@ -299,6 +300,7 @@
         while arrived < needed:
             sends[arrived].wait_recv()
             arrived += 1
+        blocks = needed - 16 - done
         rowcount = blocks * 128
         slots = []
         for i in range(blocks):
@@ -523,20 +525,17 @@
             pltpu.VMEM((16, 128, 1024), BF16),
             pltpu.VMEM((WINDOW, 128, 1024), BF16),
             pltpu.VMEM((18, 128, 1024), BF16),
-            pltpu.VMEM((2, 128, 1024), BF16),
-            pltpu.VMEM((2, 128, 1024), BF16),
-            pltpu.VMEM((2, 128, 1024), BF16),
-            pltpu.VMEM((2, 128, 1024), BF16),
-            pltpu.VMEM((2, 128, 1024), BF16),
-            pltpu.VMEM((2, 128, 1024), BF16),
+            pltpu.VMEM((4, 128, 1024), BF16),
+            pltpu.VMEM((4, 128, 1024), BF16),
+            pltpu.VMEM((4, 128, 1024), BF16),
             pltpu.VMEM((2, 128, 1024), BF16),
             pltpu.VMEM((16, 128, 2048), BF16),
             pltpu.VMEM((16, 2, 32, 2048), BF16),
             pltpu.VMEM((16, 2, 32, 2048), BF16),
             pltpu.VMEM((1024, 2048), F32),
-            pltpu.VMEM((256, 1024), BF16),
-            pltpu.VMEM((1024, 256), BF16),
-            pltpu.VMEM((256, 128), F32),
+            pltpu.VMEM((512, 1024), BF16),
+            pltpu.VMEM((1024, 512), BF16),
+            pltpu.VMEM((512, 128), F32),
             pltpu.VMEM((32, 8, 128), jnp.int32),
             pltpu.SMEM((32, 8, 128), jnp.int32),
             pltpu.SMEM((48,), jnp.int32),
@@ -585,10 +584,22 @@
     )(counts, dest, dslot, segments, tokens, cotangent, master, momentum, variance)
 
 
-def settle(w_in, m_in, l_in, w_out, m_out, l_out):
-    w_out[...] = w_in[...]
-    m_out[...] = m_in[...]
-    l_out[...] = l_in[...]
+def settle(w_in, m_in, l_in, w_out, m_out, l_out, w_mid, m_mid, l_mid, in_sem, out_sem):
+    moves = []
+    for i in range(4):
+        rows = pl.ds(i * 256, 256)
+        moves.append((w_in.at[rows], w_mid.at[rows], w_out.at[rows]))
+    moves.append((m_in, m_mid, m_out))
+    moves.append((l_in, l_mid, l_out))
+    reads = [pltpu.make_async_copy(s, m, in_sem.at[i]) for i, (s, m, d) in enumerate(moves)]
+    writes = [pltpu.make_async_copy(m, d, out_sem.at[i]) for i, (s, m, d) in enumerate(moves)]
+    for cp in reads:
+        cp.start()
+    for read, write in zip(reads, writes):
+        read.wait()
+        write.start()
+    for cp in writes:
+        cp.wait()
 
 
 def per_device(
@@ -613,17 +624,24 @@
         momentum,
         variance,
     )
-    specs = [pl.BlockSpec((rows, 2048), lambda i: (i, 0)) for rows in (256, 8, 8)]
+    hbm = pl.BlockSpec(memory_space=pl.ANY)
     return pl.pallas_call(
         settle,
-        grid=(4,),
         out_shape=(
             jax.ShapeDtypeStruct((1024, 2048), BF16),
             jax.ShapeDtypeStruct((32, 2048), F32),
             jax.ShapeDtypeStruct((32, 2048), F32),
         ),
-        in_specs=specs,
-        out_specs=tuple(specs),
+        in_specs=[hbm] * 3,
+        out_specs=(hbm,) * 3,
+        scratch_shapes=[
+            pltpu.VMEM((1024, 2048), BF16),
+            pltpu.VMEM((32, 2048), F32),
+            pltpu.VMEM((32, 2048), F32),
+            pltpu.SemaphoreType.DMA((6,)),
+            pltpu.SemaphoreType.DMA((6,)),
+        ],
+        compiler_params=pltpu.CompilerParams(vmem_limit_bytes=60 * 2**20),
         cost_estimate=pl.CostEstimate(flops=0, bytes_accessed=9 * 10**6, transcendentals=0),
     )(new_w.reshape(1024, 2048), new_m, step)
 

time: 195 us -> 188 us (0.964)
  Pallas kernels: 194 us -> 187 us
    pallas_call x1, Pallas kernels: 189 us -> 184 us  [run(): pl.pallas_call(kernel, out_shape=(jax.ShapeDtypeStruct((16, 2, 32, 2048),...]
where the time goes in v5:
time: 188 us
  Pallas kernels  187 us (99%)
    pallas_call x1, Pallas kernels, run(): pl.pallas_call(kernel, out_shape=(jax.ShapeDtypeStruct((16, 2, 32, 2048),...  184 us

profile of v5, /device:TPU:1, one launch (start us, length us, event | category | flops | bytes accessed | tf_op | source)
XLA Modules:
  0.0 188.2 jit_solution(5488515102279036234)
XLA Ops:
  0.6 183.8 %shard_map.112 = (bf16[16,2,32,2048]{3,2,1,0:T(8,128)(2,1)}, f32[32,2048]{1,0:T(8,128)}, f32[32,2048]{1,0:T(8,128)}) custom-call(s32[4]{0:T(128)} %counts.1, s32[16]{0:T(128)} %dest.1, s32[16]{0:T(128)} %dslot.1, s32[4,512]{1,0:T(4,128)} %segments.1, bf16[16,128,1024]{2,1,0:T(8,128)(2,1)} %bitcast.5, bf16[16,128,2048]{2,1,0:T(8,128)(2,1)} %bitcast.4, ...), custom_call_target="tpu_custom_call" | custom-call | flops 17999998976 | bytes 40000000 | tf_op jit(solution)/shard_map/pallas_call | solution.py:505
  184.5 3.5 %shard_map.113 = (bf16[1024,2048]{1,0:T(8,128)(2,1)}, f32[32,2048]{1,0:T(8,128)}, f32[32,2048]{1,0:T(8,128)}) custom-call(bf16[1024,2048]{1,0:T(8,128)(2,1)} %bitcast.3, f32[32,2048]{1,0:T(8,128)} %get-tuple-element.7.m_in, f32[32,2048]{1,0:T(8,128)} %get-tuple-element.8.l_in), custom_call_target="tpu_custom_call" | custom-call | bytes 9000000 | tf_op jit(solution)/shard_map/pallas_call | solution.py:628

commit v6 on v5

--- a/solution.py
+++ b/solution.py
@@ -465,6 +465,15 @@
     def _(i):
         update(place(a, i), c)
 
+    def take(ai):
+        @pl.loop(0, 4)
+        def _(i):
+            yx = ai * sb + ((a + i) % 4) * sa
+            theirs = gathered.at[yx, 1 - c]
+            copy(theirs, theirs, gcs.at[1, yx], gcr.at[1, yx], other).wait_recv()
+            update(yx, 1 - c)
+
+    pending = b
     for k in (1, 3, 2):
         ai = (a - k + 4) % 4
 
@@ -475,13 +484,14 @@
                 group(ai, bi), group(ai, bi), gas.at[1, k - 1, bi], gar.at[1, k - 1, bi], at_a(k)
             ).wait_recv()
             to_core(ai, bi)
-            update(place(ai, bi), c)
-
-    @pl.loop(0, 16)
-    def _(i):
-        theirs = gathered.at[i, 1 - c]
-        copy(theirs, theirs, gcs.at[1, i], gcr.at[1, i], other).wait_recv()
-        update(i, 1 - c)
+
+        @pl.loop(0, 4)
+        def _(i):
+            update(place(ai, i), c)
+
+        take(pending)
+        pending = (b - k + 4) % 4
+    take(pending)
 
     for cp in dcopies:
         cp.wait_send()

time: 188 us -> 188 us (level)
  no operation moved by 1% of the time
where the time goes in v6:
time: 188 us
  Pallas kernels  187 us (99%)
    pallas_call x1, Pallas kernels, run(): pl.pallas_call(kernel, out_shape=(jax.ShapeDtypeStruct((16, 2, 32, 2048),...  184 us

profile of v6, /device:TPU:1, one launch (start us, length us, event | category | flops | bytes accessed | tf_op | source)
XLA Modules:
  0.0 188.1 jit_solution(12219783702033554490)
XLA Ops:
  0.6 183.7 %shard_map.112 = (bf16[16,2,32,2048]{3,2,1,0:T(8,128)(2,1)}, f32[32,2048]{1,0:T(8,128)}, f32[32,2048]{1,0:T(8,128)}) custom-call(s32[4]{0:T(128)} %counts.1, s32[16]{0:T(128)} %dest.1, s32[16]{0:T(128)} %dslot.1, s32[4,512]{1,0:T(4,128)} %segments.1, bf16[16,128,1024]{2,1,0:T(8,128)(2,1)} %bitcast.5, bf16[16,128,2048]{2,1,0:T(8,128)(2,1)} %bitcast.4, ...), custom_call_target="tpu_custom_call" | custom-call | flops 17999998976 | bytes 40000000 | tf_op jit(solution)/shard_map/pallas_call | solution.py:515
  184.3 3.5 %shard_map.113 = (bf16[1024,2048]{1,0:T(8,128)(2,1)}, f32[32,2048]{1,0:T(8,128)}, f32[32,2048]{1,0:T(8,128)}) custom-call(bf16[1024,2048]{1,0:T(8,128)(2,1)} %bitcast.3, f32[32,2048]{1,0:T(8,128)} %get-tuple-element.7.m_in, f32[32,2048]{1,0:T(8,128)} %get-tuple-element.8.l_in), custom_call_target="tpu_custom_call" | custom-call | bytes 9000000 | tf_op jit(solution)/shard_map/pallas_call | solution.py:638
